TPU v7x, 128 devices: a whole 4x4x4 slice. The times are simulated.
128 devices in a mesh: ctx: 8 (over z, core), dp: 16 (over y, x).
Axes of the slice: x: 4, y: 4, z: 4, core: 2. Of those that a mesh axis runs over, the one named last changes fastest.
Arguments:
- hidden_in: bfloat16 [16, 1024, 2048], P('dp', 'ctx'), may hold values from -6 to 6
- queries: bfloat16 [16, 1024, 1024], P('dp', 'ctx'), may hold values from -6 to 6
- key_vectors: bfloat16 [16, 1024, 1024], P('dp', 'ctx'), may hold values from -6 to 6
- value_rows: bfloat16 [16, 1024, 2048], P('dp', 'ctx'), may hold values from -6 to 6
- out_gate: bfloat16 [16, 1024, 2048], P('dp', 'ctx'), may hold values from -6 to 6
- beta_rate: float32 [16, 1024, 16], P('dp', 'ctx'), may hold values from 0.02 to 0.25
- log_decay: float32 [16, 1024, 16], P('dp', 'ctx'), may hold values from -1 to 0
- head_gain: float32 [128], replicated, may hold values from 0.1 to 1.9
- out_proj: bfloat16 [2048, 2048], replicated, may hold values from -0.125 to 0.125
- moe_gain: float32 [2048], replicated, may hold values from 0.1 to 1.9
- router: bfloat16 [2048, 32], replicated, may hold values from -0.125 to 0.125
- expert_ids: int32 [16, 1024, 10], P('dp', 'ctx'), may hold values from 0 to 31, all different within a row; in each aligned block of 128 rows (0 to 127, 128 to 255, ..., all dimensions but the last counted through in order) at most 80 rows name the same one
- expert_in: bfloat16 [32, 2, 2048, 512], P('dp'), may hold values from -0.125 to 0.125
- expert_down: bfloat16 [32, 512, 2048], P('dp'), may hold values from -0.75 to 0.75
Outputs:
- layer_out: bfloat16 [16, 1024, 2048], P('dp', 'ctx')
Inputs may be any that keep to these rules, and one draw needn't show every extreme that they name: `expert_ids`: each position names 10 different experts. Within the rows of one device (aligned blocks of 128 positions of one sequence) no expert is named by more than 80 rows, a bound that some block reaches.
All inputs are finite; a program needn't handle non-finite values.
Results may differ from a plain program's by a relative error of at most 0.015.
Values may be sent and summed in bfloat16 or wider, within the bound.
A program may use at most 128 MiB of HBM per device.

v0:
```python
import jax
import jax.numpy as jnp
from jax import lax
from jax.sharding import PartitionSpec as P

DK = 128
DV = 128
TOP = 10
SPAN = 64


HIGHEST = lax.Precision.HIGHEST


def from_behind(value, axis, steps):
    count = lax.axis_size(axis)
    leading, last = (max(0, -steps), min(count, count - steps))
    return lax.ppermute(value, axis, [(source, source + steps) for source in range(leading, last)])


def unit_rows(matrix):
    return matrix * lax.rsqrt(jnp.sum(matrix * matrix, axis=-1, keepdims=True) + 1e-06)


def compose(earlier, later):
    first_map, first_add = earlier
    second_map, second_add = later
    joined_map = jnp.einsum("hij,hjk->hik", second_map, first_map, precision=HIGHEST)
    joined_add = jnp.einsum("hij,hjk->hik", second_map, first_add, precision=HIGHEST) + second_add
    return (joined_map, joined_add)


def per_device(
    hidden_in,
    queries,
    key_vectors,
    value_rows,
    out_gate,
    beta_rate,
    log_decay,
    head_gain,
    out_proj,
    moe_gain,
    router,
    expert_ids,
    expert_in,
    expert_down,
):
    tok_rows = hidden_in.shape[1]
    width = hidden_in.shape[2]
    key_heads = queries.shape[2] // DK
    heads = value_rows.shape[2] // DV
    group = heads // key_heads
    blocks = tok_rows // SPAN

    def by_head(array, count, size):
        return array[0].astype(jnp.float32).reshape(blocks, SPAN, count, size).transpose(2, 0, 1, 3)

    qnorm = jnp.repeat(unit_rows(by_head(queries, key_heads, DK)), group, axis=0)
    knorm = jnp.repeat(unit_rows(by_head(key_vectors, key_heads, DK)), group, axis=0)
    vnorm = by_head(value_rows, heads, DV)
    betas = beta_rate[0].reshape(blocks, SPAN, heads).transpose(2, 0, 1)
    cumul = jnp.cumsum(log_decay[0].reshape(blocks, SPAN, heads).transpose(2, 0, 1), axis=2)
    lower = jnp.arange(SPAN)[:, None] >= jnp.arange(SPAN)[None, :]
    strict = jnp.arange(SPAN)[:, None] > jnp.arange(SPAN)[None, :]
    spread = cumul[..., :, None] - cumul[..., None, :]
    ratio = jnp.where(lower, jnp.exp(jnp.where(lower, spread, 0.0)), 0.0)
    key_inner = jnp.einsum("hncd,hned->hnce", knorm, knorm, precision=HIGHEST)
    negated = -jnp.where(strict, betas[..., None] * ratio * key_inner, 0.0)
    inverse = jnp.eye(SPAN, dtype=jnp.float32) + negated
    power = negated
    for round_index in range((SPAN - 1).bit_length() - 1):
        power = jnp.einsum("hnij,hnjk->hnik", power, power, precision=HIGHEST)
        inverse = inverse + jnp.einsum("hnij,hnjk->hnik", inverse, power, precision=HIGHEST)
    growth = jnp.exp(cumul)
    value_part = jnp.einsum("hnij,hnjd->hnid", inverse, betas[..., None] * vnorm, precision=HIGHEST)
    key_part = jnp.einsum(
        "hnij,hnjd->hnid", inverse, (betas * growth)[..., None] * knorm, precision=HIGHEST
    )
    tail_keys = jnp.exp(cumul[..., -1:] - cumul)[..., None] * knorm
    eye_key = jnp.eye(DK, dtype=jnp.float32)
    span_map = growth[..., -1][..., None, None] * eye_key - jnp.einsum(
        "hncd,hnce->hnde", tail_keys, key_part, precision=HIGHEST
    )
    span_add = jnp.einsum("hncd,hnce->hnde", tail_keys, value_part, precision=HIGHEST)
    map_steps = span_map.transpose(1, 0, 2, 3)
    add_steps = span_add.transpose(1, 0, 2, 3)

    def fold_span(carried, pieces):
        return (compose(carried, pieces), None)

    identity = (jnp.broadcast_to(eye_key, (heads, DK, DK)), jnp.zeros((heads, DK, DV), jnp.float32))
    (device_map, device_add), unused_fold = lax.scan(fold_span, identity, (map_steps, add_steps))

    def pass_on(sweep_index, incoming):
        outgoing = jnp.einsum("hij,hjk->hik", device_map, incoming, precision=HIGHEST) + device_add
        return from_behind(outgoing.astype(jnp.bfloat16), "ctx", 1).astype(outgoing.dtype)

    incoming = lax.fori_loop(
        0, lax.axis_size("ctx") - 1, pass_on, jnp.zeros((heads, DK, DV), jnp.float32)
    )

    def advance_span(state, pieces):
        step_map, step_add = pieces
        return (jnp.einsum("hij,hjk->hik", step_map, state, precision=HIGHEST) + step_add, state)

    unused_end, starts = lax.scan(advance_span, incoming, (map_steps, add_steps))
    starts = starts.transpose(1, 0, 2, 3)
    corrected = value_part - jnp.einsum("hncd,hnde->hnce", key_part, starts, precision=HIGHEST)
    query_inner = jnp.einsum("hncd,hned->hnce", qnorm, knorm, precision=HIGHEST) * ratio
    core = growth[..., None] * jnp.einsum("hncd,hnde->hnce", qnorm, starts, precision=HIGHEST)
    core = core + jnp.einsum("hnij,hnjd->hnid", query_inner, corrected, precision=HIGHEST)
    scale = lax.rsqrt(jnp.mean(core * core, axis=-1, keepdims=True) + 1e-06)
    gate_heads = jax.nn.silu(by_head(out_gate, heads, DV))
    gated = (core * scale * head_gain * gate_heads).astype(jnp.bfloat16)
    gated = gated.transpose(1, 2, 0, 3).reshape(tok_rows, heads * DV)
    mixed = hidden_in[0].astype(jnp.float32) + jnp.dot(
        gated, out_proj, preferred_element_type=jnp.float32
    )
    normed = (
        mixed * lax.rsqrt(jnp.mean(mixed * mixed, axis=-1, keepdims=True) + 1e-06) * moe_gain
    ).astype(jnp.bfloat16)
    logits = jnp.dot(normed, router, preferred_element_type=jnp.float32)
    experts_all = router.shape[1]
    chosen = expert_ids[0]
    onehot = chosen[:, :, None] == jnp.arange(experts_all, dtype=jnp.int32)[None, None, :]
    picked = jnp.sum(jnp.where(onehot, logits[:, None, :], 0.0), axis=2)
    sigmas = jax.nn.sigmoid(picked)
    gates = sigmas / jnp.sum(sigmas, axis=1, keepdims=True)
    flat_hot = onehot.reshape(tok_rows * TOP, experts_all).astype(jnp.int32)
    before = jnp.cumsum(flat_hot, axis=0) - flat_hot
    slot = jnp.sum(before * flat_hot, axis=1)
    capacity = min(tok_rows, 2 * TOP * tok_rows // experts_all)
    target = chosen.reshape(-1) * capacity + slot
    buffer = (
        jnp.zeros((experts_all * capacity, width), jnp.bfloat16)
        .at[target]
        .set(jnp.repeat(normed, TOP, axis=0))
    )
    devices = lax.axis_size("dp")
    local_experts = expert_in.shape[0]
    tiles = buffer.reshape(devices, local_experts, capacity, width)
    arrived = lax.all_to_all(tiles, "dp", split_axis=0, concat_axis=0, tiled=True)
    gate_part = jnp.einsum(
        "secd,edf->secf", arrived, expert_in[:, 0], preferred_element_type=jnp.float32
    )
    up_part = jnp.einsum(
        "secd,edf->secf", arrived, expert_in[:, 1], preferred_element_type=jnp.float32
    )
    inner = (jax.nn.silu(gate_part) * up_part).astype(jnp.bfloat16)
    returned = lax.all_to_all(
        jnp.einsum("secf,efd->secd", inner, expert_down, preferred_element_type=jnp.float32).astype(
            jnp.bfloat16
        ),
        "dp",
        split_axis=0,
        concat_axis=0,
        tiled=True,
    )
    results = returned.reshape(experts_all * capacity, width)[target].reshape(tok_rows, TOP, width)
    moe_sum = jnp.sum(gates[..., None] * results.astype(jnp.float32), axis=1)
    return (mixed + moe_sum).astype(jnp.bfloat16)[None]


def solution(mesh):
    in_specs = (
        P("dp", "ctx", None),
        P("dp", "ctx", None),
        P("dp", "ctx", None),
        P("dp", "ctx", None),
        P("dp", "ctx", None),
        P("dp", "ctx", None),
        P("dp", "ctx", None),
        P(),
        P(),
        P(),
        P(),
        P("dp", "ctx", None),
        P("dp", None, None, None),
        P("dp", None, None),
    )
    out_specs = P("dp", "ctx", None)
    return jax.shard_map(
        per_device, mesh=mesh, in_specs=in_specs, out_specs=out_specs, check_vma=False
    )
```

profile of v0, /device:TPU:64, one launch (start us, length us, event | category | flops | bytes accessed | tf_op | source)
XLA Modules:
  0.0 608.7 jit_solution(15707049301032550336)
XLA Ops:
  7.7 2.8 convolution_multiply_fusion
  10.5 1.9 fusion.44
  14.8 1.3 convolution_add_fusion.8
  18.5 1.4 fusion.75
  25.1 1.4 fusion.49
  28.4 4.2 bitcast_subtract_fusion
  32.8 3.5 convolution_bitcast_fusion
  36.4 1.5 copy.117
  38.0 11.7 %while.37 = (s32[]{:T(128)}, f32[16,128,128]{2,1,0:T(8,128)S(1)}, f32[16,128,128]{2,1,0:T(8,128)}, f32[2,16,128,128]{3,2,1,0:T(8,128)S(1)}, f32[2,16,128,128]{3,2,1,0:T(8,128)}, /*index=5*/s32[]{:T(128)}, s32[]{:T(128)}) while((s32[]{:T(128)}, f32[16,128,128]{2,1,0:T(8,128)S(1)}, f32[16,128,128]{2,1,0:T(8,128)}, ...), condition=%wide.region_4.5_spmd.clone, body=%wide.region_3.4_spmd.clone.sunk | while | flops 805830656 | bytes 11535970 | solution.py:93
  39.3 3.3 convolution_add_fusion.12
  45.1 3.3 convolution_add_fusion.12
  49.7 115.4 %while.38 = (s32[]{:T(128)}, f32[16,128,128]{2,1,0:T(8,128)}, f32[16,128,128]{2,1,0:T(8,128)S(1)}, f32[16,128,128]{2,1,0:T(8,128)}, s32[]{:T(128)}, /*index=5*/s32[]{:T(128)}) while((s32[]{:T(128)}, f32[16,128,128]{2,1,0:T(8,128)}, f32[16,128,128]{2,1,0:T(8,128)S(1)}, f32[16,128,128]{2,1,0:T(8,128)}, s32[]{:T(128)}, ...), condition=%wide.region_6.7_spmd.clone, body=%wide.region_5.6_spmd.clone.sunk | while | flops 403701760 | bytes 7340151 | solution.py:99
  49.7 3.2 fusion.140
  52.9 1.9 collective-permute-start
  54.8 8.9 %collective-permute-done = bf16[16,128,128]{2,1,0:T(8,128)(2,1)} collective-permute-done((bf16[16,128,128]{2,1,0:T(8,128)(2,1)}, bf16[16,128,128]{2,1,0:T(8,128)(2,1)}, u32[]{:S(2)}, u32[]{:S(2)}) %collective-permute-start) | collective-permute-done | bytes 524320 | tf_op jit(solution)/shard_map/while/body/eval_jaxpr/ppermute | solution.py:18
  63.7 2.2 convert_element_type.123
  65.9 3.5 fusion.140
  69.4 1.9 collective-permute-start
  71.4 8.9 %collective-permute-done = bf16[16,128,128]{2,1,0:T(8,128)(2,1)} collective-permute-done((bf16[16,128,128]{2,1,0:T(8,128)(2,1)}, bf16[16,128,128]{2,1,0:T(8,128)(2,1)}, u32[]{:S(2)}, u32[]{:S(2)}) %collective-permute-start) | collective-permute-done | bytes 524320 | tf_op jit(solution)/shard_map/while/body/eval_jaxpr/ppermute | solution.py:18
  80.2 2.2 convert_element_type.123
  82.5 3.5 fusion.140
  86.0 1.9 collective-permute-start
  87.9 8.9 %collective-permute-done = bf16[16,128,128]{2,1,0:T(8,128)(2,1)} collective-permute-done((bf16[16,128,128]{2,1,0:T(8,128)(2,1)}, bf16[16,128,128]{2,1,0:T(8,128)(2,1)}, u32[]{:S(2)}, u32[]{:S(2)}) %collective-permute-start) | collective-permute-done | bytes 524320 | tf_op jit(solution)/shard_map/while/body/eval_jaxpr/ppermute | solution.py:18
  96.8 2.2 convert_element_type.123
  99.0 3.5 fusion.140
  102.5 1.9 collective-permute-start
  104.4 8.9 %collective-permute-done = bf16[16,128,128]{2,1,0:T(8,128)(2,1)} collective-permute-done((bf16[16,128,128]{2,1,0:T(8,128)(2,1)}, bf16[16,128,128]{2,1,0:T(8,128)(2,1)}, u32[]{:S(2)}, u32[]{:S(2)}) %collective-permute-start) | collective-permute-done | bytes 524320 | tf_op jit(solution)/shard_map/while/body/eval_jaxpr/ppermute | solution.py:18
  113.3 2.2 convert_element_type.123
  115.5 3.5 fusion.140
  119.0 1.9 collective-permute-start
  120.9 8.9 %collective-permute-done = bf16[16,128,128]{2,1,0:T(8,128)(2,1)} collective-permute-done((bf16[16,128,128]{2,1,0:T(8,128)(2,1)}, bf16[16,128,128]{2,1,0:T(8,128)(2,1)}, u32[]{:S(2)}, u32[]{:S(2)}) %collective-permute-start) | collective-permute-done | bytes 524320 | tf_op jit(solution)/shard_map/while/body/eval_jaxpr/ppermute | solution.py:18
  129.8 2.2 convert_element_type.123
  132.0 3.5 fusion.140
  135.6 1.9 collective-permute-start
  137.5 8.9 %collective-permute-done = bf16[16,128,128]{2,1,0:T(8,128)(2,1)} collective-permute-done((bf16[16,128,128]{2,1,0:T(8,128)(2,1)}, bf16[16,128,128]{2,1,0:T(8,128)(2,1)}, u32[]{:S(2)}, u32[]{:S(2)}) %collective-permute-start) | collective-permute-done | bytes 524320 | tf_op jit(solution)/shard_map/while/body/eval_jaxpr/ppermute | solution.py:18
  146.4 2.2 convert_element_type.123
  148.6 3.5 fusion.140
  152.1 1.9 collective-permute-start
  154.0 8.9 %collective-permute-done = bf16[16,128,128]{2,1,0:T(8,128)(2,1)} collective-permute-done((bf16[16,128,128]{2,1,0:T(8,128)(2,1)}, bf16[16,128,128]{2,1,0:T(8,128)(2,1)}, u32[]{:S(2)}, u32[]{:S(2)}) %collective-permute-start) | collective-permute-done | bytes 524320 | tf_op jit(solution)/shard_map/while/body/eval_jaxpr/ppermute | solution.py:18
  162.9 2.2 convert_element_type.123
  165.1 11.8 %while.36 = (s32[]{:T(128)}, f32[16,128,128]{2,1,0:T(8,128)}, f32[2,16,128,128]{3,2,1,0:T(8,128)}, f32[2,16,128,128]{3,2,1,0:T(8,128)S(1)}, f32[2,16,128,128]{3,2,1,0:T(8,128)}, /*index=5*/s32[]{:T(128)}) while((s32[]{:T(128)}, f32[16,128,128]{2,1,0:T(8,128)}, f32[2,16,128,128]{3,2,1,0:T(8,128)}, f32[2,16,128,128]{3,2,1,0:T(8,128)S(1)}, ...), condition=%wide.region_8.9_spmd, body=%wide.region_7.8_spmd.sunk | while | flops 402915328 | bytes 8389713 | solution.py:107
  167.5 3.5 convolution_add_fusion.11
  173.3 3.5 convolution_add_fusion.11
  176.9 5.0 fusion.40
  182.0 2.1 fusion.38
  186.3 15.9 %reduce-window.6 = s32[32,10,128]{2,1,0:T(8,128)S(1)} reduce-window(s32[32,10,128]{2,1,0:T(8,128)} %fusion.63, s32[]{:T(128)} %constant.34.clone.1), window={size=1x1x128 pad=0_0x0_0x127_0}, to_apply=%region_13.14 | reduce-window | flops 5201920 | bytes 327684 | tf_op jit(solution)/shard_map/reduce-window
  203.0 1.7 copy.130
  206.0 1.4 copy.131
  207.4 1.6 broadcast_add_fusion
  210.4 1.6 multiply_reduce_fusion.2
  213.3 4.8 multiply_reduce_fusion.1
  218.3 4.3 broadcast_in_dim.88
  222.6 9.9 %reshape.191 = bf16[1280,2048]{1,0:T(8,128)(2,1)} reshape(bf16[128,10,2048]{2,1,0:T(8,128)(2,1)} %broadcast_in_dim.88) | data formatting | bytes 10485760 | tf_op jit(solution)/shard_map/reshape | solution.py:138
  232.6 17.1 %scatter_custom_fusion = bf16[2560,2048]{1,0:T(8,128)(2,1)} fusion(s32[1280]{0:T(1024)S(1)} %fusion.69, bf16[1280,2048]{1,0:T(8,128)(2,1)} %reshape.191, bf16[]{:T(256)} %constant.54.clone.1), kind=kCustom, calls=%fused_computation.38 | custom fusion | bytes 10486272 | tf_op jit(solution)/shard_map/scatter | solution.py:138
  249.7 126.0 %all_to_all.10 = bf16[16,2,80,2048]{3,2,1,0:T(8,128)(2,1)S(1)} all-to-all(bf16[16,2,80,2048]{3,2,1,0:T(8,128)(2,1)} %bitcast.254), channel_id=1, replica_groups=mesh['ctx'=8,'dp'=16] {'dp'}, dimensions={0} | all-to-all | bytes 20971520 | tf_op jit(solution)/shard_map/all_to_all | solution.py:143
  375.7 9.0 %fusion.19 = f32[2,16,80,512]{3,2,1,0:T(8,128)} fusion(bf16[16,2,80,2048]{3,2,1,0:T(8,128)(2,1)S(1)} %all_to_all.10, bf16[2,2,2048,512]{3,2,1,0:T(8,128)(2,1)} %param.32), kind=kOutput, calls=%fused_computation.27 | convolution fusion | flops 5368709120 | bytes 19922944 | tf_op jit(solution)/shard_map/secd,edf->secf/dot_general | solution.py:147
  384.7 7.2 %fusion.21 = f32[2,16,80,512]{3,2,1,0:T(8,128)} fusion(bf16[16,2,80,2048]{3,2,1,0:T(8,128)(2,1)S(1)} %all_to_all.10, bf16[2,2,2048,512]{3,2,1,0:T(8,128)(2,1)S(1)} %bitcast.274), kind=kOutput, calls=%fused_computation.29 | convolution fusion | flops 5368709120 | bytes 19922944 | tf_op jit(solution)/shard_map/secd,edf->secf/dot_general | solution.py:144
  391.9 12.4 %convert_bitcast_fusion = bf16[16,2,80,2048]{3,2,0,1:T(8,128)(2,1)} fusion(bf16[2,512,2048]{2,1,0:T(8,128)(2,1)S(1)} %copy-done.19, f32[2,16,80,512]{3,2,1,0:T(8,128)} %fusion.19, f32[2,16,80,512]{3,2,1,0:T(8,128)} %fusion.21), kind=kOutput, calls=%fused_computation.26 | convolution fusion | flops 5381816320 | bytes 25165824 | tf_op jit(solution)/shard_map/secf,efd->secd/dot_general | solution.py:152
  404.4 10.0 %copy.136 = bf16[16,2,80,2048]{3,2,1,0:T(8,128)(2,1)} copy(bf16[16,2,80,2048]{3,2,0,1:T(8,128)(2,1)} %convert_bitcast_fusion) | data formatting | bytes 20971520 | tf_op jit(solution)/shard_map/convert_element_type | solution.py:152
  414.4 5.3 all-to-all-start.1
  420.2 151.0 %all-to-all-done.1 = bf16[16,2,80,2048]{3,2,1,0:T(8,128)(2,1)} async-done(((bf16[16,2,80,2048]{3,2,1,0:T(8,128)(2,1)}), bf16[16,2,80,2048]{3,2,1,0:T(8,128)(2,1)}, u32[]{:S(2)}, u32[]{:S(2)}) %all-to-all-start.1) | async-done | bytes 10485792 | tf_op jit(solution)/shard_map/all_to_all | solution.py:151
  571.2 16.2 %gather_fusion = bf16[1280,2048]{1,0:T(8,128)(2,1)} fusion(bf16[2560,2048]{1,0:T(8,128)(2,1)} %bitcast.33, s32[2048]{0:T(1024)S(1)} %pad_clamp_fusion), kind=kCustom, calls=%fused_computation | custom fusion | bytes 10490880 | tf_op jit(solution)/shard_map/gather | solution.py:160
  587.3 10.4 %reshape.175 = f32[128,10,2048]{2,1,0:T(8,128)} reshape(bf16[1280,2048]{1,0:T(8,128)(2,1)} %gather_fusion) | data formatting | bytes 15728640 | tf_op jit(solution)/shard_map/convert_element_type | solution.py:161
  597.7 9.5 %multiply_reduce_fusion = f32[128,2048]{1,0:T(8,128)S(1)} fusion(f32[128,10,2048]{2,1,0:T(8,128)} %reshape.175, f32[128,10]{1,0:T(8,128)S(1)} %copy.126), kind=kLoop, calls=%fused_computation.25 | loop fusion | flops 4980736 | bytes 11539456 | tf_op jit(solution)/shard_map/reduce_sum | solution.py:161
  (130 shorter events, 37.9 us)
Async XLA Ops:
  0.0 419.7 %copy-start = (bf16[2048,32]{0,1:T(8,128)(2,1)S(1)}, bf16[2048,32]{0,1:T(8,128)(2,1)}, u32[]{:S(2)}) copy-start(bf16[2048,32]{0,1:T(8,128)(2,1)} %param.30) | copy-start | bytes 393220
  0.0 6.7 %copy-start.12 = (bf16[1,128,1024]{2,1,0:T(8,128)(2,1)S(1)}, bf16[1,128,1024]{2,1,0:T(8,128)(2,1)}, u32[]{:S(2)}) copy-start(bf16[1,128,1024]{2,1,0:T(8,128)(2,1)} %param.22) | copy-start | bytes 786436
  7.6 2.9 copy-start.4
  20.0 3.6 copy-start.10
  26.6 6.2 %copy-start.1 = (f32[16,2,64,128]{3,2,1,0:T(8,128)}, f32[16,2,64,128]{3,2,1,0:T(8,128)S(1)}, u32[]{:S(2)}) copy-start(f32[16,2,64,128]{3,2,1,0:T(8,128)S(1)} %fusion.49) | copy-start | bytes 3145732
  28.4 7.9 %copy-start.3 = (f32[16,2,64,128]{3,2,1,0:T(8,128)}, f32[16,2,64,128]{3,2,1,0:T(8,128)S(1)}, u32[]{:S(2)}) copy-start(f32[16,2,64,128]{3,2,1,0:T(8,128)S(1)} %fusion.77) | copy-start | bytes 3145732
  52.9 10.8 %collective-permute-start = (bf16[16,128,128]{2,1,0:T(8,128)(2,1)}, bf16[16,128,128]{2,1,0:T(8,128)(2,1)}, u32[]{:S(2)}, u32[]{:S(2)}) collective-permute-start(bf16[16,128,128]{2,1,0:T(8,128)(2,1)} %fusion.140), channel_id=1, source_target_pairs={{0,16},{16,32},{32,48},{48,64},{64,80},{80,96},{96,112},{1,17},{17... | collective-permute-start | bytes 1572872 | tf_op jit(solution)/shard_map/while/body/eval_jaxpr/ppermute | solution.py:18
  69.4 10.8 %collective-permute-start = (bf16[16,128,128]{2,1,0:T(8,128)(2,1)}, bf16[16,128,128]{2,1,0:T(8,128)(2,1)}, u32[]{:S(2)}, u32[]{:S(2)}) collective-permute-start(bf16[16,128,128]{2,1,0:T(8,128)(2,1)} %fusion.140), channel_id=1, source_target_pairs={{0,16},{16,32},{32,48},{48,64},{64,80},{80,96},{96,112},{1,17},{17... | collective-permute-start | bytes 1572872 | tf_op jit(solution)/shard_map/while/body/eval_jaxpr/ppermute | solution.py:18
  86.0 10.8 %collective-permute-start = (bf16[16,128,128]{2,1,0:T(8,128)(2,1)}, bf16[16,128,128]{2,1,0:T(8,128)(2,1)}, u32[]{:S(2)}, u32[]{:S(2)}) collective-permute-start(bf16[16,128,128]{2,1,0:T(8,128)(2,1)} %fusion.140), channel_id=1, source_target_pairs={{0,16},{16,32},{32,48},{48,64},{64,80},{80,96},{96,112},{1,17},{17... | collective-permute-start | bytes 1572872 | tf_op jit(solution)/shard_map/while/body/eval_jaxpr/ppermute | solution.py:18
  102.5 10.8 %collective-permute-start = (bf16[16,128,128]{2,1,0:T(8,128)(2,1)}, bf16[16,128,128]{2,1,0:T(8,128)(2,1)}, u32[]{:S(2)}, u32[]{:S(2)}) collective-permute-start(bf16[16,128,128]{2,1,0:T(8,128)(2,1)} %fusion.140), channel_id=1, source_target_pairs={{0,16},{16,32},{32,48},{48,64},{64,80},{80,96},{96,112},{1,17},{17... | collective-permute-start | bytes 1572872 | tf_op jit(solution)/shard_map/while/body/eval_jaxpr/ppermute | solution.py:18
  119.0 10.8 %collective-permute-start = (bf16[16,128,128]{2,1,0:T(8,128)(2,1)}, bf16[16,128,128]{2,1,0:T(8,128)(2,1)}, u32[]{:S(2)}, u32[]{:S(2)}) collective-permute-start(bf16[16,128,128]{2,1,0:T(8,128)(2,1)} %fusion.140), channel_id=1, source_target_pairs={{0,16},{16,32},{32,48},{48,64},{64,80},{80,96},{96,112},{1,17},{17... | collective-permute-start | bytes 1572872 | tf_op jit(solution)/shard_map/while/body/eval_jaxpr/ppermute | solution.py:18
  135.6 10.8 %collective-permute-start = (bf16[16,128,128]{2,1,0:T(8,128)(2,1)}, bf16[16,128,128]{2,1,0:T(8,128)(2,1)}, u32[]{:S(2)}, u32[]{:S(2)}) collective-permute-start(bf16[16,128,128]{2,1,0:T(8,128)(2,1)} %fusion.140), channel_id=1, source_target_pairs={{0,16},{16,32},{32,48},{48,64},{64,80},{80,96},{96,112},{1,17},{17... | collective-permute-start | bytes 1572872 | tf_op jit(solution)/shard_map/while/body/eval_jaxpr/ppermute | solution.py:18
  152.1 10.8 %collective-permute-start = (bf16[16,128,128]{2,1,0:T(8,128)(2,1)}, bf16[16,128,128]{2,1,0:T(8,128)(2,1)}, u32[]{:S(2)}, u32[]{:S(2)}) collective-permute-start(bf16[16,128,128]{2,1,0:T(8,128)(2,1)} %fusion.140), channel_id=1, source_target_pairs={{0,16},{16,32},{32,48},{48,64},{64,80},{80,96},{96,112},{1,17},{17... | collective-permute-start | bytes 1572872 | tf_op jit(solution)/shard_map/while/body/eval_jaxpr/ppermute | solution.py:18
  165.1 11.8 %copy-start.2 = (f32[16,2,64,128]{3,2,1,0:T(8,128)S(1)}, f32[16,2,64,128]{3,2,1,0:T(8,128)}, u32[]{:S(2)}) copy-start(f32[16,2,64,128]{3,2,1,0:T(8,128)} %copy-done.1) | copy-start | bytes 3145732
  176.9 5.0 copy-start.5
  176.9 5.0 copy-start.6
  182.0 28.4 %copy-start.7 = (f32[16,2,64,64]{3,2,1,0:T(8,128)S(1)}, f32[16,2,64,64]{3,2,1,0:T(8,128)}, u32[]{:S(2)}) copy-start(f32[16,2,64,64]{3,2,1,0:T(8,128)} %convolution_multiply_fusion) | copy-start | bytes 1572868
  182.0 28.4 %copy-start.8 = (f32[16,2,64,128]{3,2,1,0:T(8,128)S(1)}, f32[16,2,64,128]{3,2,1,0:T(8,128)}, u32[]{:S(2)}) copy-start(f32[16,2,64,128]{3,2,1,0:T(8,128)} %fusion.40) | copy-start | bytes 3145732
  207.4 4.6 copy-start.13
  207.4 4.6 copy-start.18
  210.1 3.1 copy-start.11
  213.3 4.8 copy-start.17
  222.6 9.9 %copy-start.9 = (s32[32,10,128]{2,1,0:T(8,128)S(1)}, s32[32,10,128]{2,1,0:T(8,128)}, u32[]{:S(2)}) copy-start(s32[32,10,128]{2,1,0:T(8,128)} %broadcast_add_fusion) | copy-start | bytes 491524
  222.6 9.9 %copy-start.15 = (s32[1280]{0:T(1024)S(1)}, s32[1280]{0:T(1024)}, u32[]{:S(2)}) copy-start(s32[1280]{0:T(1024)} %eq.56) | copy-start | bytes 15364
  222.6 10.0 %copy-start.16 = (s32[1280,1]{0,1:T(1,128)S(1)}, s32[1280,1]{0,1:T(1,128)}, u32[]{:S(2)}) copy-start(s32[1280,1]{0,1:T(1,128)} %mul.218) | copy-start | bytes 15364
  249.6 135.0 %slice-start = ((s8[8388608]{0:T(1024)(128)(4,1)}), s8[4194304]{0:T(1024)(128)(4,1)S(1)}, s32[]{:S(2)}) async-start(s8[8388608]{0:T(1024)(128)(4,1)} %bitcast.273), calls=%async_computation.2 | async-start | bytes 8388608
  375.7 9.0 %slice-start.1 = ((s8[8388608]{0:T(1024)(128)(4,1)}), s8[4194304]{0:T(1024)(128)(4,1)S(1)}, s32[]{:S(2)}) async-start(s8[8388608]{0:T(1024)(128)(4,1)} %bitcast.273), calls=%async_computation.3 | async-start | bytes 8388608
  384.7 7.3 %copy-start.19 = (bf16[2,512,2048]{2,1,0:T(8,128)(2,1)S(1)}, bf16[2,512,2048]{2,1,0:T(8,128)(2,1)}, u32[]{:S(2)}) copy-start(bf16[2,512,2048]{2,1,0:T(8,128)(2,1)} %param.33) | copy-start | bytes 12582916
  414.4 5.3 copy-start.14
  414.4 156.8 %all-to-all-start.1 = ((bf16[16,2,80,2048]{3,2,1,0:T(8,128)(2,1)}), bf16[16,2,80,2048]{3,2,1,0:T(8,128)(2,1)}, u32[]{:S(2)}, u32[]{:S(2)}) async-start(bf16[16,2,80,2048]{3,2,1,0:T(8,128)(2,1)} %copy.136), calls=%async_computation.1 | async-start | bytes 20971520 | tf_op jit(solution)/shard_map/all_to_all | solution.py:151
where the time goes:
time: 620 us; the launch traced here: 609 us
  waiting for transfers between devices  213 us (34%)
  blocking collectives  126 us (20%)
  matrix products  110 us (18%)
  local copies, waits for them, and re-layouts  87.6 us (14%)
  other arithmetic  51.8 us (8%)
  starting transfers between devices  18.6 us (3%)
    all_to_all x1, waiting for transfers between devices, per_device(): lax.all_to_all(jnp.einsum('secf,efd->secd', inner, expert_down, preferred...  151 us
    all_to_all x1, blocking collectives, per_device(): lax.all_to_all(tiles, 'dp', split_axis=0, concat_axis=0, tiled=True)  126 us
    ppermute x7, waiting for transfers between devices, from_behind(): lax.ppermute(value, axis, [(source, source + steps) for source in range(l...  62.2 us
    dot_general x7, matrix products, pass_on(): jnp.einsum('hij,hjk->hik', device_map, incoming, precision=HIGHEST)  24.2 us
    another operation x3, other arithmetic  18.8 us
    scatter x1, local copies, waits for them, and re-layouts, per_device(): buffer = jnp.zeros((experts_all * capacity, width), jnp.bfloat16).at[targ...  17.1 us
    gather x1, local copies, waits for them, and re-layouts, per_device(): returned.reshape(experts_all * capacity, width)[target]  16.2 us
    convert_element_type x7, other arithmetic, pass_on(): from_behind(outgoing.astype(jnp.bfloat16), 'ctx', 1).astype(outgoing.dtype)  15.5 us
  transfers between devices with their start and end apart: 8, of which 8 were waited for; matrix products, arithmetic and copies ran while one was open for 0% of the time, Pallas kernels for 0%

commit v1 on v0

v1 whole, which is shorter than its diff:
```python
import functools

import jax
import jax.numpy as jnp
from jax import lax
from jax.experimental import pallas as pl
from jax.experimental.pallas import tpu as pltpu
from jax.sharding import PartitionSpec as P

DK = 128
DV = 128
SIDE = 4
HIGHEST = lax.Precision.HIGHEST
F32 = jnp.float32
BF16 = jnp.bfloat16


def dot_nn(a, b):
    return lax.dot_general(a, b, (((1,), (0,)), ((), ())), preferred_element_type=F32)


def dot_nt(a, b):
    return lax.dot_general(a, b, (((1,), (1,)), ((), ())), preferred_element_type=F32)


def dot_tn(a, b):
    return lax.dot_general(a, b, (((0,), (0,)), ((), ())), preferred_element_type=F32)


def unit_rows(matrix):
    return matrix * lax.rsqrt(jnp.sum(matrix * matrix, axis=-1, keepdims=True) + 1e-06)


HEADS_STEP = 4


def mixer_kernel(
    q_ref,
    k_ref,
    v_ref,
    z_ref,
    beta_ref,
    decay_ref,
    hidden_ref,
    head_gain_ref,
    moe_gain_ref,
    router_ref,
    ids_ref,
    proj_hbm,
    mixed_ref,
    normed_ref,
    proj_ref,
    cum_ref,
    add_ref,
    map_ref,
    growth_ref,
    core_add_ref,
    core_map_ref,
    state_in_ref,
    state_out_ref,
    acc_ref,
    proj_sem,
    send_sem,
    recv_sem,
):
    ctx = lax.axis_index("ctx")
    last = lax.axis_size("ctx") - 1
    tokens = q_ref.shape[0]
    heads = v_ref.shape[1] // DV
    groups = heads // HEADS_STEP
    barrier = pltpu.get_barrier_semaphore()

    for step in (1, last):
        pl.semaphore_signal(
            barrier, inc=1, device_id={"ctx": lax.rem(ctx + step, last + 1)}, device_id_type=pl.DeviceIdType.MESH
        )
    proj_copy = pltpu.make_async_copy(proj_hbm, proj_ref, proj_sem)
    proj_copy.start()

    rows = lax.broadcasted_iota(jnp.int32, (tokens, tokens), 0)
    cols = lax.broadcasted_iota(jnp.int32, (tokens, tokens), 1)
    lower = rows >= cols
    head_lane = lax.broadcasted_iota(jnp.int32, (tokens, heads), 1)
    cumul = lax.dot_general(
        lower.astype(F32), decay_ref[...], (((1,), (0,)), ((), ())),
        preferred_element_type=F32, precision=HIGHEST,
    )
    cum_ref[...] = cumul.T

    pl.semaphore_wait(barrier, 2)

    def chain_copy(group):
        part = pl.ds(group * HEADS_STEP, HEADS_STEP)
        return pltpu.make_async_remote_copy(
            src_ref=state_out_ref.at[part],
            dst_ref=state_in_ref.at[part],
            send_sem=send_sem.at[group],
            recv_sem=recv_sem.at[group],
            device_id={"ctx": lax.rem(ctx + 1, last + 1)},
            device_id_type=pl.DeviceIdType.MESH,
        )

    def local_group(group, carry):
        xs, lows, ratios, kns, qks, uses = [], [], [], [], [], []
        for pair in range(HEADS_STEP // 2):
            lanes = pl.ds(pl.multiple_of((group * (HEADS_STEP // 2) + pair) * DK, DK), DK)
            kn = unit_rows(k_ref[:, lanes].astype(F32))
            qn = unit_rows(q_ref[:, lanes].astype(F32))
            knb, qnb = kn.astype(BF16), qn.astype(BF16)
            kk, qk = dot_nt(knb, knb), dot_nt(qnb, knb)
            for half in range(2):
                head = group * HEADS_STEP + pair * 2 + half
                pick = head_lane == head
                beta = jnp.sum(jnp.where(pick, beta_ref[...], 0.0), axis=1, keepdims=True)
                cc = jnp.sum(jnp.where(pick, cumul, 0.0), axis=1, keepdims=True)
                cr = cum_ref[pl.ds(head, 1), :]
                ratio = jnp.where(lower, jnp.exp(jnp.minimum(cc - cr, 0.0)), 0.0)
                low = jnp.where(rows > cols, beta * ratio * kk, 0.0)
                xs.append(
                    jnp.where(rows == cols, 1.0, jnp.where(rows // 2 == cols // 2, -low, 0.0)).astype(BF16)
                )
                lows.append(low.astype(BF16))
                growth = jnp.exp(cc)
                end = cr[:, tokens - 1 : tokens]
                tail = (jnp.exp(end - cc) * kn).astype(BF16)
                vv = v_ref[:, pl.ds(pl.multiple_of(head * DV, DV), DV)].astype(F32)
                rhs = jnp.concatenate([beta * vv, (beta * growth) * kn], axis=1).astype(BF16)
                uses.append((head, rhs, tail, (qk * ratio).astype(BF16), growth * qn, jnp.exp(end)))
        size = 2
        while size < tokens:
            shift = size.bit_length()
            mask = ((rows >> shift) == (cols >> shift)) & ((rows >> (shift - 1)) != (cols >> (shift - 1)))
            zero = jnp.zeros((tokens, tokens), BF16)
            ys = [dot_nn(jnp.where(mask, low, zero), x).astype(BF16) for low, x in zip(lows, xs)]
            xs = [(x.astype(F32) - dot_nn(x, y)).astype(BF16) for x, y in zip(xs, ys)]
            size *= 2
        for x, (head, rhs, tail, inner, grown, end) in zip(xs, uses):
            uw = dot_nn(x, rhs).astype(BF16)
            both = dot_tn(tail, uw)
            add_ref[head] = both[:, :DV]
            map_ref[head] = both[:, DV:].astype(BF16)
            growth_ref[head] = jnp.broadcast_to(end, (8, DV))
            core = dot_nn(inner, uw)
            core_add_ref[head] = core[:, :DV]
            core_map_ref[head] = (grown - core[:, DV:]).astype(BF16)

            @pl.when(ctx == 0)
            def first_state():
                state_out_ref[head] = both[:, :DV].astype(BF16)
                state_in_ref[head] = jnp.zeros((DK, DV), BF16)

        @pl.when(ctx == 0)
        def first_send():
            chain_copy(group).start()

        return carry

    lax.fori_loop(0, groups, local_group, 0)
    proj_copy.wait()
    acc_ref[...] = hidden_ref[...].astype(F32)

    def finish_group(group, carry):
        @pl.when(ctx > 0)
        def receive():
            chain_copy(group).wait_recv()

        @pl.when((ctx > 0) & (ctx < last))
        def forward():
            for step in range(HEADS_STEP):
                head = group * HEADS_STEP + step
                state = state_in_ref[head]
                grown = growth_ref[head][0:1, :] * state.astype(F32)
                state_out_ref[head] = (grown - dot_nn(map_ref[head], state) + add_ref[head]).astype(BF16)
            chain_copy(group).start()

        pieces = []
        for step in range(HEADS_STEP):
            head = group * HEADS_STEP + step
            core = core_add_ref[head] + dot_nn(core_map_ref[head], state_in_ref[head])
            scale = lax.rsqrt(jnp.mean(core * core, axis=-1, keepdims=True) + 1e-06)
            zz = z_ref[:, pl.ds(pl.multiple_of(head * DV, DV), DV)].astype(F32)
            act = zz / (1.0 + jnp.exp(-zz))
            pieces.append((core * scale * head_gain_ref[...] * act).astype(BF16))
        gated = jnp.concatenate(pieces, axis=1)
        width = HEADS_STEP * DV
        acc_ref[...] += dot_nn(gated, proj_ref[pl.ds(pl.multiple_of(group * width, width), width), :])
        return carry

    lax.fori_loop(0, groups, finish_group, 0)
    mixed = acc_ref[...]
    mixed_ref[...] = mixed
    scale = lax.rsqrt(jnp.mean(mixed * mixed, axis=-1, keepdims=True) + 1e-06)
    normed = (mixed * scale * moe_gain_ref[...]).astype(BF16)
    logits = dot_nn(normed, router_ref[...])
    experts = router_ref.shape[1]
    lane = lax.broadcasted_iota(jnp.int32, (tokens, experts), 1)
    ids = ids_ref[...]
    chosen = lane == ids[:, 0:1]
    for k in range(1, ids.shape[1]):
        chosen = chosen | (lane == ids[:, k : k + 1])
    sigmas = jnp.where(chosen, 1.0 / (1.0 + jnp.exp(-logits)), 0.0)
    gates = sigmas / jnp.sum(sigmas, axis=1, keepdims=True)
    high = gates.astype(BF16)
    lows = (gates - high.astype(F32)).astype(BF16)
    width = mixed.shape[1]
    normed_ref[:, :width] = normed
    normed_ref[:, width:] = jnp.concatenate(
        [high, lows, jnp.zeros((tokens, 128 - 2 * experts), BF16)], axis=1
    )

    @pl.when(ctx < last)
    def drain():
        def one(group, carry):
            chain_copy(group).wait_send()
            return carry

        lax.fori_loop(0, groups, one, 0)


def mixer(q, k, v, z, beta, decay, hidden, head_gain, moe_gain, router, ids, proj):
    tokens, width = hidden.shape
    heads = v.shape[1] // DV
    vmem = pl.BlockSpec(memory_space=pltpu.VMEM)
    return pl.pallas_call(
        mixer_kernel,
        out_shape=(
            jax.ShapeDtypeStruct((tokens, width), F32),
            jax.ShapeDtypeStruct((tokens, width + 128), BF16),
        ),
        in_specs=[vmem] * 11 + [pl.BlockSpec(memory_space=pl.ANY)],
        out_specs=(vmem, vmem),
        scratch_shapes=[
            pltpu.VMEM(proj.shape, BF16),
            pltpu.VMEM((heads, tokens), F32),
            pltpu.VMEM((heads, DK, DV), F32),
            pltpu.VMEM((heads, DK, DV), BF16),
            pltpu.VMEM((heads, 8, DV), F32),
            pltpu.VMEM((heads, tokens, DV), F32),
            pltpu.VMEM((heads, tokens, DV), BF16),
            pltpu.VMEM((heads, DK, DV), BF16),
            pltpu.VMEM((heads, DK, DV), BF16),
            pltpu.VMEM((tokens, width), F32),
            pltpu.SemaphoreType.DMA,
            pltpu.SemaphoreType.DMA((heads // HEADS_STEP,)),
            pltpu.SemaphoreType.DMA((heads // HEADS_STEP,)),
        ],
        compiler_params=pltpu.CompilerParams(
            collective_id=0, has_side_effects=True, vmem_limit_bytes=40 * 1024 * 1024
        ),
    )(q, k, v, z, beta, decay, hidden, head_gain, moe_gain, router, ids, proj)


def moe_kernel(
    normed_ref,
    mixed_ref,
    win_hbm,
    wdown_hbm,
    out_ref,
    win_ref,
    wdown_ref,
    rows_ref,
    part_ref,
    far_ref,
    near_ref,
    inner_ref,
    w_sem,
    ag_send,
    ag_recv,
    rs_send,
    rs_recv,
):
    width = mixed_ref.shape[1]
    tokens = mixed_ref.shape[0]
    sub = tokens // 4
    local = win_ref.shape[0]
    experts = local * lax.axis_size("dp")
    dp = lax.axis_index("dp")
    row, col = dp // SIDE, lax.rem(dp, SIDE)

    def beside(dr, dc):
        return lax.rem(row + dr + SIDE, SIDE) * SIDE + lax.rem(col + dc + SIDE, SIDE)

    right, left, down, up = beside(0, 1), beside(0, -1), beside(1, 0), beside(-1, 0)
    first_axis = (right, left, down, up)
    second_axis = (down, up, right, left)

    barrier = pltpu.get_barrier_semaphore()
    for target in first_axis:
        pl.semaphore_signal(barrier, inc=1, device_id={"dp": target}, device_id_type=pl.DeviceIdType.MESH)
    in_copy = pltpu.make_async_copy(win_hbm, win_ref, w_sem.at[0])
    down_copy = pltpu.make_async_copy(wdown_hbm, wdown_ref, w_sem.at[1])
    for part in range(4):
        rows_ref[0, pl.ds(part * 4 * sub, sub), :] = normed_ref[pl.ds(part * sub, sub), :]
    pl.semaphore_wait(barrier, 4)

    def at(part, j):
        start = (part * 4 + j) * sub
        return pl.ds(start if isinstance(start, int) else pl.multiple_of(start, sub), sub)

    def remote(src, dst, send, recv, target):
        return pltpu.make_async_remote_copy(
            src_ref=src, dst_ref=dst, send_sem=send, recv_sem=recv,
            device_id={"dp": target}, device_id_type=pl.DeviceIdType.MESH,
        )

    def gather_copy(part, k, j, axis):
        nk, nj = (0, j + 1) if axis == 0 else (k + 1, j)
        slot = j if axis == 0 else 3 + k * 4 + j
        return remote(
            rows_ref.at[k, at(part, j)],
            rows_ref.at[nk, at(part, nj)],
            ag_send.at[part * 15 + slot],
            ag_recv.at[part * 15 + slot],
            first_axis[part] if axis == 0 else second_axis[part],
        )

    def gather_first(j):
        for part in range(4):
            gather_copy(part, 0, j - 1, 0).wait_recv()
            if j < 3:
                gather_copy(part, 0, j, 0).start()
        for part in range(4):
            gather_copy(part, 0, j, 1).start()

    def gather_second(k, j):
        for part in range(4):
            gather_copy(part, k - 1, j, 1).wait_recv()

            def onward():
                gather_copy(part, k, j, 1).start()

            if isinstance(k, int):
                if k < 3:
                    onward()
            else:
                pl.when(k < 3)(onward)

    def far_copy(part, k, j):
        return remote(
            part_ref.at[k, at(part, j)],
            far_ref.at[k - 1, at(part, j)],
            rs_send.at[part * 15 + (k - 1) * 4 + j],
            rs_recv.at[part * 15 + (k - 1) * 4 + j],
            second_axis[part],
        )

    def near_copy(part, j):
        return remote(
            part_ref.at[0, at(part, j)],
            near_ref.at[j - 1, pl.ds(part * sub, sub)],
            rs_send.at[part * 15 + 12 + j - 1],
            rs_recv.at[part * 15 + 12 + j - 1],
            first_axis[part],
        )

    def ffn_slice(k, s):
        e, half = s // 2, lax.rem(s, 2)
        quarter = win_ref.shape[3] // 2
        lanes = pl.ds(pl.multiple_of(half * quarter, quarter), quarter)
        x = rows_ref[k, :, :width]
        gate_part = dot_nn(x, win_ref[e, 0, :, lanes])
        up_part = dot_nn(x, win_ref[e, 1, :, lanes])
        extra = rows_ref[k, :, width:].astype(F32)
        lane = lax.broadcasted_iota(jnp.int32, extra.shape, 1)
        mine = dp * local + e
        pick = (lane == mine) | (lane == mine + experts)
        gate = jnp.sum(jnp.where(pick, extra, 0.0), axis=1, keepdims=True)
        inner = gate_part / (1.0 + jnp.exp(-gate_part)) * up_part * gate
        inner_ref[:, pl.ds(pl.multiple_of(s * quarter, quarter), quarter)] = inner.astype(BF16)

    def ffn_down(k):
        hidden = wdown_ref.shape[1]

        def tile(n, carry):
            lanes = pl.ds(pl.multiple_of(n * 256, 256), 256)
            total = dot_nn(inner_ref[:, :hidden], wdown_ref[0, :, lanes])
            for e in range(1, local):
                total += dot_nn(inner_ref[:, e * hidden : (e + 1) * hidden], wdown_ref[e, :, lanes])
            part_ref[k, :, lanes] = total.astype(BF16)
            return carry

        lax.fori_loop(0, width // 256, tile, 0)

    def far_step(k, j):
        for part in range(4):
            far_copy(part, k - 1, j).wait_recv()
            part_ref[k, at(part, j), :] = (
                part_ref[k, at(part, j), :].astype(F32) + far_ref[k - 2, at(part, j), :].astype(F32)
            ).astype(BF16)
            far_copy(part, k, j).start()

    for part in range(4):
        gather_copy(part, 0, 0, 0).start()
    for part in range(4):
        gather_copy(part, 0, 0, 1).start()
    in_copy.start()
    down_copy.start()
    gather_first(1)
    gather_second(1, 0)
    gather_first(2)
    gather_second(1, 1)
    gather_first(3)
    in_copy.wait()
    down_copy.wait()

    def step(i, carry):
        k, s = i // 4, lax.rem(i, 4)

        @pl.when((k == 0) & (s < 2))
        def early():
            gather_second(1, s + 2)

        @pl.when((k == 1) | (k == 2))
        def middle():
            gather_second(k + 1, s)

        @pl.when(k == 3)
        def late():
            far_step(2, lax.rem(s + 1, 4))

        ffn_slice(k, s)

        @pl.when(s == 3)
        def last_slice():
            ffn_down(k)

            @pl.when(k == 1)
            def first_sums():
                for j in (1, 2, 3, 0):
                    for part in range(4):
                        far_copy(part, 1, j).start()

        return carry

    lax.fori_loop(0, 16, step, 0)

    def third(j, carry):
        far_step(3, lax.rem(j + 1, 4))
        return carry

    lax.fori_loop(0, 4, third, 0)
    for j in (1, 2, 3, 0):
        for part in range(4):
            far_copy(part, 3, j).wait_recv()
            total = part_ref[0, at(part, j), :].astype(F32) + far_ref[2, at(part, j), :].astype(F32)
            if j != 1:
                came = (j + 3) % 4
                near_copy(part, came).wait_recv()
                total = total + near_ref[came - 1, pl.ds(part * sub, sub), :].astype(F32)
            if j != 0:
                part_ref[0, at(part, j), :] = total.astype(BF16)
                near_copy(part, j).start()
            else:
                span = pl.ds(part * sub, sub)
                out_ref[span, :] = (mixed_ref[span, :] + total).astype(BF16)

    for part in range(4):
        for j in range(3):
            gather_copy(part, 0, j, 0).wait_send()
        for k in range(3):
            for j in range(4):
                gather_copy(part, k, j, 1).wait_send()
                far_copy(part, k + 1, j).wait_send()
        for j in range(1, 4):
            near_copy(part, j).wait_send()


def moe(normed, mixed, win, wdown):
    tokens, width = mixed.shape
    vmem = pl.BlockSpec(memory_space=pltpu.VMEM)
    anywhere = pl.BlockSpec(memory_space=pl.ANY)
    return pl.pallas_call(
        moe_kernel,
        out_shape=jax.ShapeDtypeStruct((tokens, width), BF16),
        in_specs=[vmem, vmem, anywhere, anywhere],
        out_specs=vmem,
        scratch_shapes=[
            pltpu.VMEM(win.shape, BF16),
            pltpu.VMEM(wdown.shape, BF16),
            pltpu.VMEM((4, 4 * tokens, normed.shape[1]), BF16),
            pltpu.VMEM((4, 4 * tokens, width), BF16),
            pltpu.VMEM((3, 4 * tokens, width), BF16),
            pltpu.VMEM((3, tokens, width), BF16),
            pltpu.VMEM((4 * tokens, win.shape[0] * win.shape[3]), BF16),
            pltpu.SemaphoreType.DMA((2,)),
            pltpu.SemaphoreType.DMA((60,)),
            pltpu.SemaphoreType.DMA((60,)),
            pltpu.SemaphoreType.DMA((60,)),
            pltpu.SemaphoreType.DMA((60,)),
        ],
        compiler_params=pltpu.CompilerParams(
            collective_id=1, has_side_effects=True, vmem_limit_bytes=58 * 1024 * 1024
        ),
    )(normed, mixed, win, wdown)


def per_device(
    hidden_in,
    queries,
    key_vectors,
    value_rows,
    out_gate,
    beta_rate,
    log_decay,
    head_gain,
    out_proj,
    moe_gain,
    router,
    expert_ids,
    expert_in,
    expert_down,
):
    mixed, normed = mixer(
        queries[0],
        key_vectors[0],
        value_rows[0],
        out_gate[0],
        beta_rate[0],
        log_decay[0],
        hidden_in[0],
        head_gain[None],
        moe_gain[None],
        router,
        expert_ids[0],
        out_proj,
    )
    return moe(normed, mixed, expert_in, expert_down)[None]


def solution(mesh):
    in_specs = (
        P("dp", "ctx", None),
        P("dp", "ctx", None),
        P("dp", "ctx", None),
        P("dp", "ctx", None),
        P("dp", "ctx", None),
        P("dp", "ctx", None),
        P("dp", "ctx", None),
        P(),
        P(),
        P(),
        P(),
        P("dp", "ctx", None),
        P("dp", None, None, None),
        P("dp", None, None),
    )
    out_specs = P("dp", "ctx", None)
    return jax.shard_map(
        per_device, mesh=mesh, in_specs=in_specs, out_specs=out_specs, check_vma=False
    )
```

time: 620 us -> 157 us (0.25)
  the two profiles are of different devices: /device:TPU:64 before, /device:TPU:96 now
where the time goes in v1:
time: 157 us
  Pallas kernels  140 us (89%)
  local copies, waits for them, and re-layouts  17 us (11%)
    pallas_call x1, Pallas kernels, moe(): pl.pallas_call(moe_kernel, out_shape=jax.ShapeDtypeStruct((tokens, width)...  107 us
    pallas_call x1, Pallas kernels, mixer(): pl.pallas_call(mixer_kernel, out_shape=(jax.ShapeDtypeStruct((tokens, wid...  32.2 us
    unnamed x25, local copies, waits for them, and re-layouts  17 us

profile of v1, /device:TPU:96, one launch (start us, length us, event | category | flops | bytes accessed | tf_op | source)
XLA Modules:
  0.0 156.7 jit_solution(1957084086112829415)
XLA Ops:
  0.0 0.8 copy.15
  0.8 0.8 copy.16
  1.6 0.8 copy.17
  2.4 1.2 copy.18.router_ref
  3.6 0.0 copy-start
  3.6 3.4 %copy-done = bf16[2048,2048]{1,0:T(8,128)(2,1)S(1)} copy-done((bf16[2048,2048]{1,0:T(8,128)(2,1)S(1)}, bf16[2048,2048]{1,0:T(8,128)(2,1)}, u32[]{:S(2)}) %copy-start) | copy-done | bytes 8388632
  7.0 0.0 copy-start.3
  7.0 1.0 copy-done.3
  8.0 0.0 copy-start.4
  8.0 1.0 copy-done.4
  9.0 0.0 copy-start.5
  9.0 1.0 copy-done.5
  10.1 0.0 copy-start.6
  10.1 0.9 copy-done.6
  11.0 0.0 copy-start.7
  11.0 0.9 copy-done.7
  12.0 0.0 copy-start.8
  12.0 0.7 copy-done.8
  12.7 0.0 copy-start.9
  12.7 0.7 copy-done.9
  13.3 32.2 %shard_map.136 = (f32[128,2048]{1,0:T(8,128)S(1)}, bf16[128,2176]{1,0:T(8,128)(2,1)S(1)}) custom-call(bf16[128,1024]{1,0:T(8,128)(2,1)S(1)} %bitcast.17, bf16[128,1024]{1,0:T(8,128)(2,1)S(1)} %bitcast.18, bf16[128,2048]{1,0:T(8,128)(2,1)S(1)} %bitcast.11, bf16[128,2048]{1,0:T(8,128)(2,1)S(1)} %bitcast.12, f32[128,16]{1,0:T(8,128)S(1)} %bitcast.14, ...), custom_call_target="tpu_custom_call" | custom-call | tf_op jit(solution)/shard_map/pallas_call | solution.py:224
  45.6 0.0 copy-start.1
  45.6 1.0 copy-done.1
  46.5 0.0 copy-start.2
  46.5 0.8 copy-done.2
  47.4 107.4 %shard_map.137 = bf16[128,2048]{1,0:T(8,128)(2,1)} custom-call(bf16[128,2176]{1,0:T(8,128)(2,1)} %copy-done.2, f32[128,2048]{1,0:T(8,128)} %copy-done.1, bf16[2,2,2048,512]{3,2,1,0:T(8,128)(2,1)} %win_hbm.1, bf16[2,512,2048]{2,1,0:T(8,128)(2,1)} %wdown_hbm.1), custom_call_target="tpu_custom_call" | custom-call | tf_op jit(solution)/shard_map/pallas_call | solution.py:472
  154.8 1.9 %copy.20 = bf16[1,128,2048]{2,1,0:T(8,128)(2,1)} copy(bf16[1,128,2048]{2,1,0:T(8,128)(2,1)} %bitcast.21) | data formatting | bytes 1048576
Async XLA Ops:
  3.6 3.4 %copy-start = (bf16[2048,2048]{1,0:T(8,128)(2,1)S(1)}, bf16[2048,2048]{1,0:T(8,128)(2,1)}, u32[]{:S(2)}) copy-start(bf16[2048,2048]{1,0:T(8,128)(2,1)} %proj_hbm.1) | copy-start | bytes 25165828
  7.0 1.0 copy-start.3
  8.0 1.0 copy-start.4
  9.0 1.0 copy-start.5
  10.1 0.9 copy-start.6
  11.0 0.9 copy-start.7
  12.0 0.7 copy-start.8
  12.7 0.7 copy-start.9
  45.6 1.0 copy-start.1
  46.5 0.8 copy-start.2

commit v2 on v0

v2 whole, which is shorter than its diff:
```python
import jax
import jax.numpy as jnp
from jax import lax
from jax.experimental import pallas as pl
from jax.experimental.pallas import tpu as pltpu
from jax.sharding import PartitionSpec as P

DK = 128
DV = 128
SIDE = 4
HIGHEST = lax.Precision.HIGHEST
F32 = jnp.float32
BF16 = jnp.bfloat16


def dot_nn(a, b):
    return lax.dot_general(a, b, (((1,), (0,)), ((), ())), preferred_element_type=F32)


def dot_nt(a, b):
    return lax.dot_general(a, b, (((1,), (1,)), ((), ())), preferred_element_type=F32)


def dot_tn(a, b):
    return lax.dot_general(a, b, (((0,), (0,)), ((), ())), preferred_element_type=F32)


def unit_rows(matrix):
    return matrix * lax.rsqrt(jnp.sum(matrix * matrix, axis=-1, keepdims=True) + 1e-06)


HEADS_STEP = 4
UNITS = 8
MESH = pl.DeviceIdType.MESH


def layer_kernel(
    q_hbm,
    k_hbm,
    v_hbm,
    z_hbm,
    beta_hbm,
    decay_hbm,
    hidden_hbm,
    head_gain_hbm,
    moe_gain_hbm,
    router_hbm,
    ids_hbm,
    proj_hbm,
    win_hbm,
    wdown_hbm,
    out_ref,
    q_ref,
    k_ref,
    v_ref,
    z_ref,
    beta_ref,
    decay_ref,
    hidden_ref,
    head_gain_ref,
    moe_gain_ref,
    router_ref,
    ids_ref,
    proj_ref,
    win_ref,
    wdown_ref,
    far_in_ref,
    far_down_ref,
    cum_ref,
    add_ref,
    map_ref,
    growth_ref,
    core_add_ref,
    core_map_ref,
    state_in_ref,
    state_out_ref,
    acc_ref,
    rows_ref,
    part_ref,
    xsum_ref,
    ysum_ref,
    inner_ref,
    in_sem,
    chain_send,
    chain_recv,
    fetch_send,
    fetch_recv,
    ring_send,
    ring_recv,
    share_send,
    share_recv,
    gx_send,
    gx_recv,
    gy_send,
    gy_recv,
    sx_send,
    sx_recv,
    sy_send,
    sy_recv,
):
    ctx = lax.axis_index("ctx")
    shards = lax.axis_size("ctx")
    last = shards - 1
    dp = lax.axis_index("dp")
    row, col = dp // SIDE, lax.rem(dp, SIDE)
    tokens, width = hidden_ref.shape
    heads = v_ref.shape[1] // DV
    groups = heads // HEADS_STEP
    experts = router_ref.shape[0]
    local = experts // lax.axis_size("dp")
    half = tokens // 2

    def beside(dr, dc):
        return lax.rem(row + dr + SIDE, SIDE) * SIDE + lax.rem(col + dc + SIDE, SIDE)

    def along(step):
        return lax.rem(ctx + step + shards, shards)

    right, left, down, up = beside(0, 1), beside(0, -1), beside(1, 0), beside(-1, 0)
    partner = beside(0, 2)
    sibling = ctx + 1 - 2 * lax.rem(ctx, 2)

    barrier = pltpu.get_barrier_semaphore()
    for target in (right, left, down, up, partner):
        pl.semaphore_signal(barrier, inc=1, device_id={"dp": target}, device_id_type=MESH)
    for step in (1, -1, 2, -2):
        pl.semaphore_signal(barrier, inc=1, device_id={"ctx": along(step)}, device_id_type=MESH)

    loads = [
        pltpu.make_async_copy(src, dst, in_sem.at[n])
        for n, (src, dst) in enumerate(
            (
                (decay_hbm, decay_ref),
                (beta_hbm, beta_ref),
                (k_hbm, k_ref),
                (q_hbm, q_ref),
                (v_hbm, v_ref),
                (z_hbm, z_ref),
                (hidden_hbm, hidden_ref),
                (head_gain_hbm, head_gain_ref),
                (moe_gain_hbm, moe_gain_ref),
                (router_hbm, router_ref),
                (ids_hbm, ids_ref),
                (proj_hbm, proj_ref),
                (win_hbm, win_ref),
                (wdown_hbm, wdown_ref),
            )
        )
    ]
    for load in loads[:11]:
        load.start()

    in_span = win_hbm.shape[0] // (UNITS * shards)
    down_span = wdown_hbm.shape[0] // (UNITS * shards)

    def piece(owner, u):
        n = u * shards + owner
        return (
            pl.ds(pl.multiple_of(n * in_span, in_span), in_span),
            pl.ds(pl.multiple_of(n * down_span, down_span), down_span),
        )

    class Both:
        def __init__(self, src, owner, u, send, recv, slot, target):
            spans = piece(owner, u)
            self.copies = [
                pltpu.make_async_remote_copy(
                    src_ref=ref.at[span],
                    dst_ref=dst.at[span],
                    send_sem=send.at[slot * 2 + n],
                    recv_sem=recv.at[slot * 2 + n],
                    device_id=target,
                    device_id_type=MESH,
                )
                for n, (ref, dst, span) in enumerate(zip(src, (far_in_ref, far_down_ref), spans))
            ]

        def start(self):
            for copy in self.copies:
                copy.start()

        def wait_recv(self):
            for copy in self.copies:
                copy.wait_recv()

        def wait_send(self):
            for copy in self.copies:
                copy.wait_send()

    far = (far_in_ref, far_down_ref)

    def fetch(u):
        return Both((win_hbm, wdown_hbm), ctx, u, fetch_send, fetch_recv, u, {"dp": partner})

    def ring(lane, owner, u, target):
        return Both(far, owner, u, ring_send, ring_recv, lane * UNITS + u, {"ctx": target})

    def share(lane, owner, u):
        return Both(far, owner, u, share_send, share_recv, lane * UNITS + u, {"ctx": sibling})

    def own_piece(u):
        fetch(u).wait_recv()
        ring(0, ctx, u, along(2)).start()
        ring(1, ctx, u, along(-2)).start()
        share(0, ctx, u).start()

    def ring_piece(u):
        behind, ahead = along(-2), along(2)
        ring(0, behind, u, along(2)).wait_recv()
        if u % 2 == 0:
            ring(2, behind, u, along(2)).start()
        share(1, behind, u).start()
        ring(1, ahead, u, along(-2)).wait_recv()
        if u % 2 == 1:
            ring(2, ahead, u, along(-2)).start()
        share(2, ahead, u).start()

    def ring_piece_far(u):
        ring(2, along(4), u, along(2)).wait_recv()
        share(3, along(4), u).start()

    def share_recv_all(u):
        for lane, step in enumerate((0, -2, 2, 4)):
            share(lane, lax.rem(sibling + step + shards, shards), u).wait_recv()

    pl.semaphore_wait(barrier, 9)
    for u in range(UNITS):
        fetch(u).start()
    for load in loads[11:]:
        load.start()
    for load in loads[:5]:
        load.wait()

    rows = lax.broadcasted_iota(jnp.int32, (tokens, tokens), 0)
    cols = lax.broadcasted_iota(jnp.int32, (tokens, tokens), 1)
    lower = rows >= cols
    head_lane = lax.broadcasted_iota(jnp.int32, (tokens, heads), 1)
    cum_rows = lax.dot_general(
        decay_ref[...], (rows <= cols).astype(F32), (((1,), (0,)), ((), ())),
        preferred_element_type=F32, precision=HIGHEST,
    )
    cum_ref[...] = cum_rows
    cumul = cum_rows.T
    betas = beta_ref[...].T

    def chain_copy(group):
        part = pl.ds(group * HEADS_STEP, HEADS_STEP)
        return pltpu.make_async_remote_copy(
            src_ref=state_out_ref.at[part],
            dst_ref=state_in_ref.at[part],
            send_sem=chain_send.at[group],
            recv_sem=chain_recv.at[group],
            device_id={"ctx": along(1)},
            device_id_type=MESH,
        )

    def local_group(group):
        xs, lows, uses = [], [], []
        for pair in range(HEADS_STEP // 2):
            lanes = pl.ds(pl.multiple_of((group * (HEADS_STEP // 2) + pair) * DK, DK), DK)
            kn = unit_rows(k_ref[:, lanes].astype(F32))
            qn = unit_rows(q_ref[:, lanes].astype(F32))
            knb, qnb = kn.astype(BF16), qn.astype(BF16)
            kk, qk = dot_nt(knb, knb), dot_nt(qnb, knb)
            for other in range(2):
                head = group * HEADS_STEP + pair * 2 + other
                pick = head_lane == head
                beta = jnp.sum(jnp.where(pick, betas, 0.0), axis=1, keepdims=True)
                cc = jnp.sum(jnp.where(pick, cumul, 0.0), axis=1, keepdims=True)
                cr = cum_ref[pl.ds(head, 1), :]
                ratio = jnp.where(lower, jnp.exp(jnp.minimum(cc - cr, 0.0)), 0.0)
                low = jnp.where(rows > cols, beta * ratio * kk, 0.0)
                xs.append(
                    jnp.where(rows == cols, 1.0, jnp.where(rows // 2 == cols // 2, -low, 0.0)).astype(BF16)
                )
                lows.append(low.astype(BF16))
                growth = jnp.exp(cc)
                end = cr[:, tokens - 1 : tokens]
                tail = (jnp.exp(end - cc) * kn).astype(BF16)
                vv = v_ref[:, pl.ds(pl.multiple_of(head * DV, DV), DV)].astype(F32)
                rhs = jnp.concatenate([beta * vv, (beta * growth) * kn], axis=1).astype(BF16)
                uses.append((head, rhs, tail, (qk * ratio).astype(BF16), growth * qn, jnp.exp(end)))
        size = 2
        while size < tokens:
            shift = size.bit_length()
            mask = ((rows >> shift) == (cols >> shift)) & ((rows >> (shift - 1)) != (cols >> (shift - 1)))
            zero = jnp.zeros((tokens, tokens), BF16)
            ys = [dot_nn(jnp.where(mask, low, zero), x).astype(BF16) for low, x in zip(lows, xs)]
            xs = [(x.astype(F32) - dot_nn(x, y)).astype(BF16) for x, y in zip(xs, ys)]
            size *= 2
        for x, (head, rhs, tail, inner, grown, end) in zip(xs, uses):
            uw = dot_nn(x, rhs).astype(BF16)
            both = dot_tn(tail, uw)
            add_ref[head] = both[:, :DV]
            map_ref[head] = both[:, DV:].astype(BF16)
            growth_ref[head] = jnp.broadcast_to(end, (8, DV))
            core = dot_nn(inner, uw)
            core_add_ref[head] = core[:, :DV]
            core_map_ref[head] = (grown - core[:, DV:]).astype(BF16)

            @pl.when(ctx == 0)
            def first_state():
                state_out_ref[head] = both[:, :DV].astype(BF16)
                state_in_ref[head] = jnp.zeros((DK, DV), BF16)

        @pl.when(ctx == 0)
        def first_send():
            chain_copy(group).start()

    def finish_group(group):
        @pl.when(ctx > 0)
        def receive():
            chain_copy(group).wait_recv()

        @pl.when((ctx > 0) & (ctx < last))
        def forward():
            for step in range(HEADS_STEP):
                head = group * HEADS_STEP + step
                state = state_in_ref[head]
                grown = growth_ref[head][0:1, :] * state.astype(F32)
                state_out_ref[head] = (grown - dot_nn(map_ref[head], state) + add_ref[head]).astype(BF16)
            chain_copy(group).start()

        pieces = []
        for step in range(HEADS_STEP):
            head = group * HEADS_STEP + step
            core = core_add_ref[head] + dot_nn(core_map_ref[head], state_in_ref[head])
            scale = lax.rsqrt(jnp.mean(core * core, axis=-1, keepdims=True) + 1e-06)
            zz = z_ref[:, pl.ds(pl.multiple_of(head * DV, DV), DV)].astype(F32)
            act = zz / (1.0 + jnp.exp(-zz))
            pieces.append((core * scale * head_gain_ref[...] * act).astype(BF16))
        gated = jnp.concatenate(pieces, axis=1)
        span = HEADS_STEP * DV
        acc_ref[...] += dot_nn(gated, proj_ref[pl.ds(pl.multiple_of(group * span, span), span), :])

    def local_step(group, carry):
        local_group(group)

        @pl.when(group == 1)
        def weights_a():
            own_piece(0)

        @pl.when(group == 2)
        def weights_b():
            own_piece(1)

        @pl.when(group == 3)
        def weights_c():
            own_piece(2)
            ring_piece(0)

        return carry

    lax.fori_loop(0, groups, local_step, 0)
    for load in loads[5:12]:
        load.wait()
    acc_ref[...] = hidden_ref[...].astype(F32)

    def finish_step(group, carry):
        finish_group(group)

        @pl.when(group == 0)
        def weights_a():
            own_piece(3)

        @pl.when(group == 2)
        def weights_b():
            ring_piece(1)

        return carry

    lax.fori_loop(0, groups, finish_step, 0)
    mixed = acc_ref[...]
    scale = lax.rsqrt(jnp.mean(mixed * mixed, axis=-1, keepdims=True) + 1e-06)
    normed = (mixed * scale * moe_gain_ref[...]).astype(BF16)
    logits = dot_nt(router_ref[...], normed)
    place = lax.broadcasted_iota(jnp.int32, (experts, tokens), 0)
    chosen = place == ids_ref[0]
    for k in range(1, ids_ref.shape[0]):
        chosen = chosen | (place == ids_ref[k])
    sigmas = jnp.where(chosen, 1.0 / (1.0 + jnp.exp(-logits)), 0.0)
    gates = (sigmas / jnp.sum(sigmas, axis=0, keepdims=True)).T
    high = gates.astype(BF16)
    lows = (gates - high.astype(F32)).astype(BF16)

    def own(k):
        return 2 * k - (k + 2) // 3

    def cross(k):
        return 2 * k + 2 - k // 3

    def at(slot, part):
        return pl.ds(pl.multiple_of(slot * tokens + part * half, half), half)

    rows_ref[pl.ds(0, tokens), :width] = normed
    rows_ref[pl.ds(0, tokens), width:] = jnp.concatenate(
        [high, lows, jnp.zeros((tokens, 128 - 2 * experts), BF16)], axis=1
    )

    def remote(src, dst, send, recv, target):
        return pltpu.make_async_remote_copy(
            src_ref=src, dst_ref=dst, send_sem=send, recv_sem=recv, device_id={"dp": target}, device_id_type=MESH
        )

    def gather_y(part, k):
        n = part * 3 + k
        return remote(
            rows_ref.at[at(own(k), part)], rows_ref.at[at(own(k + 1), part)],
            gy_send.at[n], gy_recv.at[n], (down, up)[part],
        )

    def gather_x(part, k):
        n = part * 4 + k
        return remote(
            rows_ref.at[at(own(k), part)], rows_ref.at[at(cross(k), part)],
            gx_send.at[n], gx_recv.at[n], (right, left)[part],
        )

    def sum_x(part, k):
        n = part * 4 + k
        return remote(
            part_ref.at[at(cross(k), part)], xsum_ref.at[at(k, part)],
            sx_send.at[n], sx_recv.at[n], (left, right)[part],
        )

    def sum_y(part, k):
        n = part * 3 + k - 1
        return remote(
            part_ref.at[at(own(k), part)], ysum_ref.at[at(k - 1, part)],
            sy_send.at[n], sy_recv.at[n], (down, up)[part],
        )

    def send_rows(k):
        for part in range(2):
            if k < 3:
                gather_y(part, k).start()
            gather_x(part, k).start()

    def take_rows(k):
        for part in range(2):
            gather_y(part, k - 1).wait_recv()
        send_rows(k)

    def take_cross(k):
        for part in range(2):
            gather_x(part, k).wait_recv()

    def ffn(start, count, in_ref, down_ref, first, number, owner, add):
        block = pl.ds(start if isinstance(start, int) else pl.multiple_of(start, tokens), count)
        hidden = down_ref.shape[0] // local
        quarter = hidden // 2

        def up_tile(n, carry):
            e = first + n // 2
            lanes = pl.ds(pl.multiple_of(lax.rem(n, 2) * quarter, quarter), quarter)
            x = rows_ref[block, :width]
            base = e * 2 * width
            gate_part = dot_nn(x, in_ref[pl.ds(pl.multiple_of(base, width), width), lanes])
            up_part = dot_nn(x, in_ref[pl.ds(pl.multiple_of(base + width, width), width), lanes])
            extra = rows_ref[block, width:].astype(F32)
            lane = lax.broadcasted_iota(jnp.int32, extra.shape, 1)
            mine = owner * local + e
            gate = jnp.sum(jnp.where((lane == mine) | (lane == mine + experts), extra, 0.0), axis=1, keepdims=True)
            inner = gate_part / (1.0 + jnp.exp(-gate_part)) * up_part * gate
            inner_ref[pl.ds(0, count), pl.ds(pl.multiple_of(n * quarter, quarter), quarter)] = inner.astype(BF16)
            return carry

        lax.fori_loop(0, 2 * number, up_tile, 0)

        def down_tile(n, carry):
            lanes = pl.ds(pl.multiple_of(n * 256, 256), 256)
            total = dot_nn(
                inner_ref[pl.ds(0, count), : number * hidden],
                down_ref[pl.ds(first * hidden, number * hidden), lanes],
            )
            if add:
                total += part_ref[block, lanes].astype(F32)
            part_ref[block, lanes] = total.astype(BF16)
            return carry

        lax.fori_loop(0, width // 256, down_tile, 0)

    def near_experts(slot, count):
        ffn(slot * tokens, count * tokens, win_ref, wdown_ref, 0, local, dp, False)

    def far_expert(slot, count, e):
        ffn(slot * tokens, count * tokens, far_in_ref, far_down_ref, e, 1, partner, True)

    send_rows(0)
    own_piece(4)
    ring_piece_far(0)
    for load in loads[12:]:
        load.wait()
    near_experts(0, 1)
    own_piece(5)
    ring_piece(2)
    ring_piece_far(1)
    take_rows(1)
    take_cross(0)

    def near_step(n, carry):
        near_experts(1 + 2 * n, 2)

        @pl.when(n == 0)
        def weights_a():
            ring_piece(3)
            own_piece(6)
            ring_piece_far(2)
            take_rows(2)
            take_cross(1)
            own_piece(7)
            ring_piece(4)

        @pl.when(n == 1)
        def weights_b():
            ring_piece_far(3)
            take_rows(3)
            take_cross(2)
            ring_piece(5)

        return carry

    lax.fori_loop(0, 3, near_step, 0)
    ring_piece_far(4)
    for u in range(UNITS // 2):
        share_recv_all(u)

    def far_first(n, carry):
        far_expert(2 * n, 2, 0)

        @pl.when(n == 0)
        def weights_a():
            ring_piece_far(5)
            ring_piece(6)

        @pl.when(n == 1)
        def weights_b():
            ring_piece_far(6)
            ring_piece(7)

        @pl.when(n == 2)
        def tail_rows():
            take_cross(3)
            near_experts(7, 1)

        return carry

    lax.fori_loop(0, 4, far_first, 0)
    ring_piece_far(7)
    for u in range(UNITS // 2, UNITS):
        share_recv_all(u)

    def far_cross(n, carry):
        k = lax.rem(n + 1, 4)
        far_expert(cross(k), 1, 1)
        for part in range(2):
            sum_x(part, k).start()
        return carry

    lax.fori_loop(0, 4, far_cross, 0)

    def far_own(n, carry):
        k = lax.rem(n + 1, 4)
        far_expert(own(k), 1, 1)
        for part in range(2):
            sum_x(part, k).wait_recv()
            spot = at(own(k), part)
            part_total = part_ref[spot, :].astype(F32) + xsum_ref[at(k, part), :].astype(F32)

            @pl.when(n == 0)
            def begin():
                part_ref[spot, :] = part_total.astype(BF16)

            @pl.when(n > 0)
            def more():
                sum_y(part, n).wait_recv()
                total = part_total + ysum_ref[at(n - 1, part), :].astype(F32)

                @pl.when(n < 3)
                def keep():
                    part_ref[spot, :] = total.astype(BF16)

                @pl.when(n == 3)
                def finish():
                    span = pl.ds(part * half, half)
                    out_ref[span, :] = (acc_ref[span, :] + total).astype(BF16)

            @pl.when(n < 3)
            def onward():
                sum_y(part, n + 1).start()

        return carry

    lax.fori_loop(0, 4, far_own, 0)

    for part in range(2):
        for k in range(4):
            gather_x(part, k).wait_send()
            sum_x(part, k).wait_send()
        for k in range(3):
            gather_y(part, k).wait_send()
            sum_y(part, k + 1).wait_send()
    for u in range(UNITS):
        fetch(u).wait_send()
        ring(0, ctx, u, along(2)).wait_send()
        ring(1, ctx, u, along(-2)).wait_send()
        ring(2, along(-2) if u % 2 == 0 else along(2), u, along(2)).wait_send()
        for lane, step in enumerate((0, -2, 2, 4)):
            share(lane, along(step), u).wait_send()

    @pl.when(ctx < last)
    def drain():
        for group in range(groups):
            chain_copy(group).wait_send()


def layer(q, k, v, z, beta, decay, hidden, head_gain, moe_gain, router, ids, proj, win, wdown):
    tokens, width = hidden.shape
    heads = v.shape[1] // DV
    args = (q, k, v, z, beta, decay, hidden, head_gain, moe_gain, router, ids, proj, win, wdown)
    hbm = pl.BlockSpec(memory_space=pltpu.HBM)
    dma = pltpu.SemaphoreType.DMA
    return pl.pallas_call(
        layer_kernel,
        out_shape=jax.ShapeDtypeStruct((tokens, width), BF16),
        in_specs=[hbm] * len(args),
        out_specs=pl.BlockSpec(memory_space=pltpu.VMEM),
        scratch_shapes=[pltpu.VMEM(arg.shape, arg.dtype) for arg in args]
        + [
            pltpu.VMEM(win.shape, BF16),
            pltpu.VMEM(wdown.shape, BF16),
            pltpu.VMEM((heads, tokens), F32),
            pltpu.VMEM((heads, DK, DV), F32),
            pltpu.VMEM((heads, DK, DV), BF16),
            pltpu.VMEM((heads, 8, DV), F32),
            pltpu.VMEM((heads, tokens, DV), F32),
            pltpu.VMEM((heads, tokens, DV), BF16),
            pltpu.VMEM((heads, DK, DV), BF16),
            pltpu.VMEM((heads, DK, DV), BF16),
            pltpu.VMEM((tokens, width), F32),
            pltpu.VMEM((8 * tokens, width + 128), BF16),
            pltpu.VMEM((8 * tokens, width), BF16),
            pltpu.VMEM((4 * tokens, width), BF16),
            pltpu.VMEM((3 * tokens, width), BF16),
            pltpu.VMEM((2 * tokens, wdown.shape[0]), BF16),
            dma((len(args),)),
            dma((heads // HEADS_STEP,)),
            dma((heads // HEADS_STEP,)),
            dma((2 * UNITS,)),
            dma((2 * UNITS,)),
            dma((6 * UNITS,)),
            dma((6 * UNITS,)),
            dma((8 * UNITS,)),
            dma((8 * UNITS,)),
            dma((8,)),
            dma((8,)),
            dma((6,)),
            dma((6,)),
            dma((8,)),
            dma((8,)),
            dma((6,)),
            dma((6,)),
        ],
        compiler_params=pltpu.CompilerParams(
            collective_id=0, has_side_effects=True, vmem_limit_bytes=62 * 1024 * 1024
        ),
    )(*args)


def per_device(
    hidden_in,
    queries,
    key_vectors,
    value_rows,
    out_gate,
    beta_rate,
    log_decay,
    head_gain,
    out_proj,
    moe_gain,
    router,
    expert_ids,
    expert_in,
    expert_down,
):
    return layer(
        queries[0],
        key_vectors[0],
        value_rows[0],
        out_gate[0],
        beta_rate[0].T,
        log_decay[0].T,
        hidden_in[0],
        head_gain[None],
        moe_gain[None],
        router.T,
        expert_ids.transpose(2, 0, 1),
        out_proj,
        expert_in.reshape(-1, expert_in.shape[-1]),
        expert_down.reshape(-1, expert_down.shape[-1]),
    )[None]


def solution(mesh):
    in_specs = (
        P("dp", "ctx", None),
        P("dp", "ctx", None),
        P("dp", "ctx", None),
        P("dp", "ctx", None),
        P("dp", "ctx", None),
        P("dp", "ctx", None),
        P("dp", "ctx", None),
        P(),
        P(),
        P(),
        P(),
        P("dp", "ctx", None),
        P("dp", None, None, None),
        P("dp", None, None),
    )
    out_specs = P("dp", "ctx", None)
    return jax.shard_map(
        per_device, mesh=mesh, in_specs=in_specs, out_specs=out_specs, check_vma=False
    )
```

time: 620 us -> 155 us (0.25)
  the two profiles are of different devices: /device:TPU:64 before, /device:TPU:1 now
where the time goes in v2:
time: 155 us
  Pallas kernels  153 us (99%)
  local copies, waits for them, and re-layouts  1.88 us (1%)
    pallas_call x1, Pallas kernels, layer(): pl.pallas_call(layer_kernel, out_shape=jax.ShapeDtypeStruct((tokens, widt...  153 us

profile of v2, /device:TPU:1, one launch (start us, length us, event | category | flops | bytes accessed | tf_op | source)
XLA Modules:
  0.0 154.8 jit_solution(17679140046189279742)
XLA Ops:
  0.0 152.9 %shard_map.136 = bf16[128,2048]{1,0:T(8,128)(2,1)} custom-call(bf16[128,1024]{1,0:T(8,128)(2,1)} %bitcast.24, bf16[128,1024]{1,0:T(8,128)(2,1)} %bitcast.25, bf16[128,2048]{1,0:T(8,128)(2,1)} %bitcast.21, bf16[128,2048]{1,0:T(8,128)(2,1)} %bitcast.22, f32[16,128]{1,0:T(8,128)} %bitcast.27, f32[16,128]{1,0:T(8,128)} %bitcast.28, bf16[128,2048]{1,0:T(8,128)(2,1)} %bitcast.23, ...), custom_call_target="tpu_custom_call" | custom-call | tf_op jit(solution)/shard_map/pallas_call | solution.py:623
  152.9 1.9 %copy.16 = bf16[1,128,2048]{2,1,0:T(8,128)(2,1)} copy(bf16[1,128,2048]{2,1,0:T(8,128)(2,1)} %bitcast.20) | data formatting | bytes 1048576

commit v3 on v2

--- a/solution.py
+++ b/solution.py
@@ -153,7 +153,7 @@
     in_span = win_hbm.shape[0] // (UNITS * shards)
     down_span = wdown_hbm.shape[0] // (UNITS * shards)
 
-    def piece(owner, u):
+    def weight_spans(owner, u):
         n = u * shards + owner
         return (
             pl.ds(pl.multiple_of(n * in_span, in_span), in_span),
@@ -162,7 +162,7 @@
 
     class Both:
         def __init__(self, src, owner, u, send, recv, slot, target):
-            spans = piece(owner, u)
+            spans = weight_spans(owner, u)
             self.copies = [
                 pltpu.make_async_remote_copy(
                     src_ref=ref.at[span],
@@ -198,26 +198,69 @@
     def share(lane, owner, u):
         return Both(far, owner, u, share_send, share_recv, lane * UNITS + u, {"ctx": sibling})
 
-    def own_piece(u):
+    depth = ctx // 2
+    top = depth == last // 2
+
+    def own_piece(u, forward):
         fetch(u).wait_recv()
-        ring(0, ctx, u, along(2)).start()
         ring(1, ctx, u, along(-2)).start()
         share(0, ctx, u).start()
-
-    def ring_piece(u):
-        behind, ahead = along(-2), along(2)
+        if forward:
+            ring(0, ctx, u, along(2)).start()
+        else:
+            pl.when(top)(ring(0, ctx, u, along(2)).start)
+
+    def piece_ahead(u):
+        ahead = along(2)
+        ring(1, ahead, u, along(-2)).wait_recv()
+
+        @pl.when(lax.rem(u, 4) > 0)
+        def onward():
+            ring(2, ahead, u, along(-2)).start()
+
+        share(2, ahead, u).start()
+
+    def piece_behind(u):
+        behind = along(-2)
         ring(0, behind, u, along(2)).wait_recv()
-        if u % 2 == 0:
+
+        @pl.when(lax.rem(u, 4) == 0)
+        def onward():
             ring(2, behind, u, along(2)).start()
+
         share(1, behind, u).start()
-        ring(1, ahead, u, along(-2)).wait_recv()
-        if u % 2 == 1:
-            ring(2, ahead, u, along(-2)).start()
-        share(2, ahead, u).start()
-
-    def ring_piece_far(u):
+
+    def piece_opposite(u):
         ring(2, along(4), u, along(2)).wait_recv()
         share(3, along(4), u).start()
+
+    rounds = UNITS + 5
+
+    def weights(since, until, forward=True):
+        def weights_round(r, carry):
+            @pl.when(r < UNITS)
+            def one():
+                own_piece(r, forward)
+
+            @pl.when((r >= 2) & (r < UNITS + 2))
+            def two():
+                piece_ahead(r - 2)
+
+            @pl.when((r >= 4) & (r < UNITS + 4))
+            def three():
+                piece_behind(r - 4)
+
+            @pl.when(r >= 5)
+            def four():
+                piece_opposite(r - 5)
+
+            return carry
+
+        lax.fori_loop(since, until, weights_round, 0)
+
+    before = jnp.maximum(depth, 1)
+    after = jnp.minimum(depth + 2, 4)
+    third = (2 * depth) // 3
 
     def share_recv_all(u):
         for lane, step in enumerate((0, -2, 2, 4)):
@@ -336,22 +379,10 @@
     def local_step(group, carry):
         local_group(group)
 
-        @pl.when(group == 1)
-        def weights_a():
-            own_piece(0)
-
-        @pl.when(group == 2)
-        def weights_b():
-            own_piece(1)
-
-        @pl.when(group == 3)
-        def weights_c():
-            own_piece(2)
-            ring_piece(0)
-
         return carry
 
     lax.fori_loop(0, groups, local_step, 0)
+    weights(0, before, False)
     for load in loads[5:12]:
         load.wait()
     acc_ref[...] = hidden_ref[...].astype(F32)
@@ -359,17 +390,15 @@
     def finish_step(group, carry):
         finish_group(group)
 
-        @pl.when(group == 0)
-        def weights_a():
-            own_piece(3)
-
-        @pl.when(group == 2)
-        def weights_b():
-            ring_piece(1)
-
         return carry
 
     lax.fori_loop(0, groups, finish_step, 0)
+
+    def late_start(u, carry):
+        ring(0, ctx, u, along(2)).start()
+        return carry
+
+    lax.fori_loop(0, jnp.where(top, 0, before), late_start, 0)
     mixed = acc_ref[...]
     scale = lax.rsqrt(jnp.mean(mixed * mixed, axis=-1, keepdims=True) + 1e-06)
     normed = (mixed * scale * moe_gain_ref[...]).astype(BF16)
@@ -383,17 +412,20 @@
     high = gates.astype(BF16)
     lows = (gates - high.astype(F32)).astype(BF16)
 
-    def own(k):
-        return 2 * k - (k + 2) // 3
-
-    def cross(k):
-        return 2 * k + 2 - k // 3
-
-    def at(slot, part):
-        return pl.ds(pl.multiple_of(slot * tokens + part * half, half), half)
-
-    rows_ref[pl.ds(0, tokens), :width] = normed
-    rows_ref[pl.ds(0, tokens), width:] = jnp.concatenate(
+    quarter = half // 2
+
+    def own(n):
+        return 2 + n + 2 * (n // 2)
+
+    def cross(n):
+        return lax.rem(n + 4, 6)
+
+    def at(slot, part, piece):
+        return pl.ds(pl.multiple_of(slot * tokens + part * half + piece * quarter, quarter), quarter)
+
+    home = pl.ds(7 * tokens, tokens)
+    rows_ref[home, :width] = normed
+    rows_ref[home, width:] = jnp.concatenate(
         [high, lows, jnp.zeros((tokens, 128 - 2 * experts), BF16)], axis=1
     )
 
@@ -402,73 +434,81 @@
             src_ref=src, dst_ref=dst, send_sem=send, recv_sem=recv, device_id={"dp": target}, device_id_type=MESH
         )
 
-    def gather_y(part, k):
-        n = part * 3 + k
+    def gather_y(part, k, piece):
+        n = (part * 3 + k) * 2 + piece
         return remote(
-            rows_ref.at[at(own(k), part)], rows_ref.at[at(own(k + 1), part)],
+            rows_ref.at[at(own(lax.rem(k + 3, 4)), part, piece)], rows_ref.at[at(own(k), part, piece)],
             gy_send.at[n], gy_recv.at[n], (down, up)[part],
         )
 
-    def gather_x(part, k):
-        n = part * 4 + k
+    def gather_x(part, k, piece):
+        n = (part * 4 + k) * 2 + piece
         return remote(
-            rows_ref.at[at(own(k), part)], rows_ref.at[at(cross(k), part)],
+            rows_ref.at[at(own(lax.rem(k + 3, 4)), part, piece)], rows_ref.at[at(cross(lax.rem(k + 3, 4)), part, piece)],
             gx_send.at[n], gx_recv.at[n], (right, left)[part],
         )
 
-    def sum_x(part, k):
-        n = part * 4 + k
+    def sum_x(part, n, piece):
+        slot = (part * 4 + n) * 2 + piece
         return remote(
-            part_ref.at[at(cross(k), part)], xsum_ref.at[at(k, part)],
-            sx_send.at[n], sx_recv.at[n], (left, right)[part],
+            part_ref.at[at(cross(n), part, piece)], xsum_ref.at[at(n, part, piece)],
+            sx_send.at[slot], sx_recv.at[slot], (left, right)[part],
         )
 
-    def sum_y(part, k):
-        n = part * 3 + k - 1
+    def sum_y(part, n, piece):
+        slot = (part * 3 + n) * 2 + piece
         return remote(
-            part_ref.at[at(own(k), part)], ysum_ref.at[at(k - 1, part)],
-            sy_send.at[n], sy_recv.at[n], (down, up)[part],
+            part_ref.at[at(own(n), part, piece)], ysum_ref.at[at(n, part, piece)],
+            sy_send.at[slot], sy_recv.at[slot], (down, up)[part],
         )
 
-    def send_rows(k):
+    def send_rows(k, piece):
         for part in range(2):
-            if k < 3:
-                gather_y(part, k).start()
-            gather_x(part, k).start()
+            if isinstance(k, int):
+                gather_y(part, k, piece).start()
+            else:
+                pl.when(k < 3)(gather_y(part, k, piece).start)
+            gather_x(part, k, piece).start()
 
     def take_rows(k):
-        for part in range(2):
-            gather_y(part, k - 1).wait_recv()
-        send_rows(k)
+        for piece in range(2):
+            for part in range(2):
+                gather_y(part, k - 1, piece).wait_recv()
+            send_rows(k, piece)
 
     def take_cross(k):
-        for part in range(2):
-            gather_x(part, k).wait_recv()
+        for piece in range(2):
+            for part in range(2):
+                gather_x(part, k, piece).wait_recv()
 
     def ffn(start, count, in_ref, down_ref, first, number, owner, add):
         block = pl.ds(start if isinstance(start, int) else pl.multiple_of(start, tokens), count)
         hidden = down_ref.shape[0] // local
-        quarter = hidden // 2
 
         def up_tile(n, carry):
-            e = first + n // 2
-            lanes = pl.ds(pl.multiple_of(lax.rem(n, 2) * quarter, quarter), quarter)
+            e = first + n
             x = rows_ref[block, :width]
             base = e * 2 * width
-            gate_part = dot_nn(x, in_ref[pl.ds(pl.multiple_of(base, width), width), lanes])
-            up_part = dot_nn(x, in_ref[pl.ds(pl.multiple_of(base + width, width), width), lanes])
+            base = base if isinstance(base, int) else pl.multiple_of(base, width)
+            gate_part = dot_nn(x, in_ref[pl.ds(base, width), :])
+            up_part = dot_nn(x, in_ref[pl.ds(base + width, width), :])
             extra = rows_ref[block, width:].astype(F32)
             lane = lax.broadcasted_iota(jnp.int32, extra.shape, 1)
             mine = owner * local + e
             gate = jnp.sum(jnp.where((lane == mine) | (lane == mine + experts), extra, 0.0), axis=1, keepdims=True)
             inner = gate_part / (1.0 + jnp.exp(-gate_part)) * up_part * gate
-            inner_ref[pl.ds(0, count), pl.ds(pl.multiple_of(n * quarter, quarter), quarter)] = inner.astype(BF16)
+            lanes = pl.ds(0 if number == 1 else pl.multiple_of(n * hidden, hidden), hidden)
+            inner_ref[pl.ds(0, count), lanes] = inner.astype(BF16)
             return carry
 
-        lax.fori_loop(0, 2 * number, up_tile, 0)
+        if number == 1:
+            up_tile(0, 0)
+        else:
+            lax.fori_loop(0, number, up_tile, 0)
+        wide = width // 2
 
         def down_tile(n, carry):
-            lanes = pl.ds(pl.multiple_of(n * 256, 256), 256)
+            lanes = pl.ds(pl.multiple_of(n * wide, wide), wide)
             total = dot_nn(
                 inner_ref[pl.ds(0, count), : number * hidden],
                 down_ref[pl.ds(first * hidden, number * hidden), lanes],
@@ -478,128 +518,116 @@
             part_ref[block, lanes] = total.astype(BF16)
             return carry
 
-        lax.fori_loop(0, width // 256, down_tile, 0)
+        lax.fori_loop(0, 2, down_tile, 0)
 
     def near_experts(slot, count):
         ffn(slot * tokens, count * tokens, win_ref, wdown_ref, 0, local, dp, False)
 
-    def far_expert(slot, count, e):
-        ffn(slot * tokens, count * tokens, far_in_ref, far_down_ref, e, 1, partner, True)
-
-    send_rows(0)
-    own_piece(4)
-    ring_piece_far(0)
+    def far_expert(slot, e):
+        ffn(slot * tokens, 2 * tokens, far_in_ref, far_down_ref, e, 1, partner, True)
+
+    send_rows(0, 0)
+    send_rows(0, 1)
+    weights(before, after)
     for load in loads[12:]:
         load.wait()
-    near_experts(0, 1)
-    own_piece(5)
-    ring_piece(2)
-    ring_piece_far(1)
+    near_experts(7, 1)
+    weights(after, 4 + depth // 2)
     take_rows(1)
     take_cross(0)
 
     def near_step(n, carry):
         near_experts(1 + 2 * n, 2)
 
-        @pl.when(n == 0)
-        def weights_a():
-            ring_piece(3)
-            own_piece(6)
-            ring_piece_far(2)
-            take_rows(2)
-            take_cross(1)
-            own_piece(7)
-            ring_piece(4)
-
-        @pl.when(n == 1)
-        def weights_b():
-            ring_piece_far(3)
-            take_rows(3)
-            take_cross(2)
-            ring_piece(5)
+        @pl.when(n < 2)
+        def more():
+            take_rows(n + 2)
+            weights(jnp.where(n == 0, 4 + depth // 2, 5 + third), 5 + n + third)
+            take_cross(n + 1)
 
         return carry
 
     lax.fori_loop(0, 3, near_step, 0)
-    ring_piece_far(4)
+    weights(6 + third, 9)
     for u in range(UNITS // 2):
         share_recv_all(u)
 
     def far_first(n, carry):
-        far_expert(2 * n, 2, 0)
-
-        @pl.when(n == 0)
-        def weights_a():
-            ring_piece_far(5)
-            ring_piece(6)
+        far_expert(lax.rem(4 + 2 * n, 8) - 2 * (n // 2) + 4 * (n // 2) - 4 * (n // 3), 0)
 
         @pl.when(n == 1)
-        def weights_b():
-            ring_piece_far(6)
-            ring_piece(7)
-
-        @pl.when(n == 2)
         def tail_rows():
             take_cross(3)
-            near_experts(7, 1)
+            near_experts(0, 1)
+
+        @pl.when(n < 3)
+        def more():
+            weights(9 + n, 10 + n)
 
         return carry
 
     lax.fori_loop(0, 4, far_first, 0)
-    ring_piece_far(7)
+    weights(12, rounds)
     for u in range(UNITS // 2, UNITS):
         share_recv_all(u)
 
     def far_cross(n, carry):
-        k = lax.rem(n + 1, 4)
-        far_expert(cross(k), 1, 1)
-        for part in range(2):
-            sum_x(part, k).start()
+        far_expert(cross(2 * n), 1)
+        for m in range(2):
+            for piece in range(2):
+                for part in range(2):
+                    sum_x(part, 2 * n + m, piece).start()
         return carry
 
-    lax.fori_loop(0, 4, far_cross, 0)
+    lax.fori_loop(0, 2, far_cross, 0)
 
     def far_own(n, carry):
-        k = lax.rem(n + 1, 4)
-        far_expert(own(k), 1, 1)
-        for part in range(2):
-            sum_x(part, k).wait_recv()
-            spot = at(own(k), part)
-            part_total = part_ref[spot, :].astype(F32) + xsum_ref[at(k, part), :].astype(F32)
-
-            @pl.when(n == 0)
-            def begin():
-                part_ref[spot, :] = part_total.astype(BF16)
-
-            @pl.when(n > 0)
-            def more():
-                sum_y(part, n).wait_recv()
-                total = part_total + ysum_ref[at(n - 1, part), :].astype(F32)
+        far_expert(own(2 * n), 1)
+        return carry
+
+    lax.fori_loop(0, 2, far_own, 0)
+
+    def collect(n, carry):
+        for piece in range(2):
+            for part in range(2):
+                sum_x(part, n, piece).wait_recv()
+                spot = at(own(n), part, piece)
+                both = part_ref[spot, :].astype(F32) + xsum_ref[at(n, part, piece), :].astype(F32)
+
+                @pl.when(n == 0)
+                def begin():
+                    part_ref[spot, :] = both.astype(BF16)
+
+                @pl.when(n > 0)
+                def more():
+                    sum_y(part, n - 1, piece).wait_recv()
+                    total = both + ysum_ref[at(n - 1, part, piece), :].astype(F32)
+
+                    @pl.when(n < 3)
+                    def keep():
+                        part_ref[spot, :] = total.astype(BF16)
+
+                    @pl.when(n == 3)
+                    def finish():
+                        span = pl.ds(part * half + piece * quarter, quarter)
+                        out_ref[span, :] = (acc_ref[span, :] + total).astype(BF16)
 
                 @pl.when(n < 3)
-                def keep():
-                    part_ref[spot, :] = total.astype(BF16)
-
-                @pl.when(n == 3)
-                def finish():
-                    span = pl.ds(part * half, half)
-                    out_ref[span, :] = (acc_ref[span, :] + total).astype(BF16)
-
-            @pl.when(n < 3)
-            def onward():
-                sum_y(part, n + 1).start()
+                def onward():
+                    sum_y(part, n, piece).start()
 
         return carry
 
-    lax.fori_loop(0, 4, far_own, 0)
+    lax.fori_loop(0, 4, collect, 0)
 
     for part in range(2):
-        for k in range(4):
-            gather_x(part, k).wait_send()
-            sum_x(part, k).wait_send()
-        for k in range(3):
-            gather_y(part, k).wait_send()
-            sum_y(part, k + 1).wait_send()
+        for piece in range(2):
+            for k in range(4):
+                gather_x(part, k, piece).wait_send()
+                sum_x(part, k, piece).wait_send()
+            for k in range(3):
+                gather_y(part, k, piece).wait_send()
+                sum_y(part, k, piece).wait_send()
     for u in range(UNITS):
         fetch(u).wait_send()
         ring(0, ctx, u, along(2)).wait_send()
@@ -652,14 +680,14 @@
             dma((6 * UNITS,)),
             dma((8 * UNITS,)),
             dma((8 * UNITS,)),
-            dma((8,)),
-            dma((8,)),
-            dma((6,)),
-            dma((6,)),
-            dma((8,)),
-            dma((8,)),
-            dma((6,)),
-            dma((6,)),
+            dma((16,)),
+            dma((16,)),
+            dma((12,)),
+            dma((12,)),
+            dma((16,)),
+            dma((16,)),
+            dma((12,)),
+            dma((12,)),
         ],
         compiler_params=pltpu.CompilerParams(
             collective_id=0, has_side_effects=True, vmem_limit_bytes=62 * 1024 * 1024

time: 155 us -> 129 us (0.83)
  Pallas kernels: 153 us -> 127 us
    pallas_call x1, Pallas kernels: 153 us -> 127 us  [layer(): pl.pallas_call(layer_kernel, out_shape=jax.ShapeDtypeStruct((tokens, widt...]
where the time goes in v3:
time: 129 us
  Pallas kernels  127 us (98%)
  local copies, waits for them, and re-layouts  1.88 us (1%)
    pallas_call x1, Pallas kernels, layer(): pl.pallas_call(layer_kernel, out_shape=jax.ShapeDtypeStruct((tokens, widt...  127 us

profile of v3, /device:TPU:1, one launch (start us, length us, event | category | flops | bytes accessed | tf_op | source)
XLA Modules:
  0.0 129.2 jit_solution(17589056793505360590)
XLA Ops:
  0.0 127.4 %shard_map.136 = bf16[128,2048]{1,0:T(8,128)(2,1)} custom-call(bf16[128,1024]{1,0:T(8,128)(2,1)} %bitcast.24, bf16[128,1024]{1,0:T(8,128)(2,1)} %bitcast.25, bf16[128,2048]{1,0:T(8,128)(2,1)} %bitcast.21, bf16[128,2048]{1,0:T(8,128)(2,1)} %bitcast.22, f32[16,128]{1,0:T(8,128)} %bitcast.27, f32[16,128]{1,0:T(8,128)} %bitcast.28, bf16[128,2048]{1,0:T(8,128)(2,1)} %bitcast.23, ...), custom_call_target="tpu_custom_call" | custom-call | tf_op jit(solution)/shard_map/pallas_call | solution.py:651
  127.4 1.9 %copy.16 = bf16[1,128,2048]{2,1,0:T(8,128)(2,1)} copy(bf16[1,128,2048]{2,1,0:T(8,128)(2,1)} %bitcast.20) | data formatting | bytes 1048576

commit v4 on v3

--- a/solution.py
+++ b/solution.py
@@ -1,3 +1,5 @@
+import functools
+
 import jax
 import jax.numpy as jnp
 from jax import lax
@@ -201,14 +203,17 @@
     depth = ctx // 2
     top = depth == last // 2
 
-    def own_piece(u, forward):
+    def early_piece(u):
         fetch(u).wait_recv()
         ring(1, ctx, u, along(-2)).start()
         share(0, ctx, u).start()
-        if forward:
-            ring(0, ctx, u, along(2)).start()
-        else:
-            pl.when(top)(ring(0, ctx, u, along(2)).start)
+        pl.when(top | (u < depth))(ring(0, ctx, u, along(2)).start)
+
+    def own_piece(u):
+        fetch(u).wait_recv()
+        ring(1, ctx, u, along(-2)).start()
+        share(0, ctx, u).start()
+        ring(0, ctx, u, along(2)).start()
 
     def piece_ahead(u):
         ahead = along(2)
@@ -234,33 +239,36 @@
         ring(2, along(4), u, along(2)).wait_recv()
         share(3, along(4), u).start()
 
-    rounds = UNITS + 5
-
-    def weights(since, until, forward=True):
-        def weights_round(r, carry):
-            @pl.when(r < UNITS)
-            def one():
-                own_piece(r, forward)
-
-            @pl.when((r >= 2) & (r < UNITS + 2))
-            def two():
-                piece_ahead(r - 2)
-
-            @pl.when((r >= 4) & (r < UNITS + 4))
-            def three():
-                piece_behind(r - 4)
-
-            @pl.when(r >= 5)
-            def four():
-                piece_opposite(r - 5)
-
-            return carry
-
-        lax.fori_loop(since, until, weights_round, 0)
-
-    before = jnp.maximum(depth, 1)
-    after = jnp.minimum(depth + 2, 4)
-    third = (2 * depth) // 3
+    kinds = (own_piece, piece_ahead, piece_behind, piece_opposite)
+
+    def weights(since, until):
+        for move, low, high in zip(kinds, since, until):
+            if low is not high:
+
+                def one(u, carry, move=move):
+                    move(u)
+                    return carry
+
+                lax.fori_loop(low, high, one, 0)
+
+    odd = (depth + 1) // 2
+    early = (depth + 3, depth + 1, 0, 0)
+    stages = (
+        (depth + 5, jnp.minimum(depth + 3, 5), 2, 0),
+        (UNITS, 4 + odd, 4, 1),
+        (UNITS, 6 + odd, 6, 4),
+        (UNITS, UNITS, 7, 5),
+        (UNITS, UNITS, UNITS, 6),
+        (UNITS, UNITS, UNITS, UNITS),
+        (UNITS, UNITS, UNITS, UNITS),
+        (UNITS, UNITS, UNITS, UNITS),
+    )
+
+    def pick(n, options):
+        return tuple(
+            functools.reduce(lambda other, m: jnp.where(n == m, options[m][kind], other), range(1, len(options)), options[0][kind])
+            for kind in range(4)
+        )
 
     def share_recv_all(u):
         for lane, step in enumerate((0, -2, 2, 4)):
@@ -382,14 +390,32 @@
         return carry
 
     lax.fori_loop(0, groups, local_step, 0)
-    weights(0, before, False)
+
+    def early_own(u, carry):
+        early_piece(u)
+        return carry
+
+    def early_ahead(u, carry):
+        piece_ahead(u)
+        return carry
+
+    before = jnp.maximum(depth, 1)
+    lax.fori_loop(0, before, early_own, 0)
     for load in loads[5:12]:
         load.wait()
     acc_ref[...] = hidden_ref[...].astype(F32)
 
     def finish_step(group, carry):
         finish_group(group)
-
+        lax.fori_loop(
+            jnp.where(group == 0, before, depth + 1 + group // 2), depth + 1 + (group + 1) // 2, early_own, 0
+        )
+        lax.fori_loop(
+            jnp.where(group < 2, 0, depth),
+            jnp.where(group == 0, 0, jnp.where(group < groups - 1, depth, depth + 1)),
+            early_ahead,
+            0,
+        )
         return carry
 
     lax.fori_loop(0, groups, finish_step, 0)
@@ -398,7 +424,7 @@
         ring(0, ctx, u, along(2)).start()
         return carry
 
-    lax.fori_loop(0, jnp.where(top, 0, before), late_start, 0)
+    lax.fori_loop(jnp.where(top, depth + 3, depth), depth + 3, late_start, 0)
     mixed = acc_ref[...]
     scale = lax.rsqrt(jnp.mean(mixed * mixed, axis=-1, keepdims=True) + 1e-06)
     normed = (mixed * scale * moe_gain_ref[...]).astype(BF16)
@@ -528,11 +554,10 @@
 
     send_rows(0, 0)
     send_rows(0, 1)
-    weights(before, after)
     for load in loads[12:]:
         load.wait()
     near_experts(7, 1)
-    weights(after, 4 + depth // 2)
+    weights(early, stages[0])
     take_rows(1)
     take_cross(0)
 
@@ -542,13 +567,13 @@
         @pl.when(n < 2)
         def more():
             take_rows(n + 2)
-            weights(jnp.where(n == 0, 4 + depth // 2, 5 + third), 5 + n + third)
+            weights(pick(n, stages[0:2]), pick(n, stages[1:3]))
             take_cross(n + 1)
 
         return carry
 
     lax.fori_loop(0, 3, near_step, 0)
-    weights(6 + third, 9)
+    weights(stages[2], stages[3])
     for u in range(UNITS // 2):
         share_recv_all(u)
 
@@ -562,12 +587,12 @@
 
         @pl.when(n < 3)
         def more():
-            weights(9 + n, 10 + n)
+            weights(pick(n, stages[3:6]), pick(n, stages[4:7]))
 
         return carry
 
     lax.fori_loop(0, 4, far_first, 0)
-    weights(12, rounds)
+    weights(stages[6], stages[7])
     for u in range(UNITS // 2, UNITS):
         share_recv_all(u)
 

time: 129 us -> 123 us (0.953)
  Pallas kernels: 127 us -> 121 us
    pallas_call x1, Pallas kernels: 127 us -> 121 us  [layer(): pl.pallas_call(layer_kernel, out_shape=jax.ShapeDtypeStruct((tokens, widt...]
where the time goes in v4:
time: 123 us
  Pallas kernels  121 us (98%)
  local copies, waits for them, and re-layouts  1.88 us (2%)
    pallas_call x1, Pallas kernels, layer(): pl.pallas_call(layer_kernel, out_shape=jax.ShapeDtypeStruct((tokens, widt...  121 us

profile of v4, /device:TPU:1, one launch (start us, length us, event | category | flops | bytes accessed | tf_op | source)
XLA Modules:
  0.0 122.6 jit_solution(15406483324703485175)
XLA Ops:
  0.0 120.7 %shard_map.136 = bf16[128,2048]{1,0:T(8,128)(2,1)} custom-call(bf16[128,1024]{1,0:T(8,128)(2,1)} %bitcast.24, bf16[128,1024]{1,0:T(8,128)(2,1)} %bitcast.25, bf16[128,2048]{1,0:T(8,128)(2,1)} %bitcast.21, bf16[128,2048]{1,0:T(8,128)(2,1)} %bitcast.22, f32[16,128]{1,0:T(8,128)} %bitcast.27, f32[16,128]{1,0:T(8,128)} %bitcast.28, bf16[128,2048]{1,0:T(8,128)(2,1)} %bitcast.23, ...), custom_call_target="tpu_custom_call" | custom-call | tf_op jit(solution)/shard_map/pallas_call | solution.py:676
  120.7 1.9 %copy.16 = bf16[1,128,2048]{2,1,0:T(8,128)(2,1)} copy(bf16[1,128,2048]{2,1,0:T(8,128)(2,1)} %bitcast.20) | data formatting | bytes 1048576

commit v5 on v4

--- a/solution.py
+++ b/solution.py
@@ -554,10 +554,12 @@
 
     send_rows(0, 0)
     send_rows(0, 1)
+    greeting = (depth + 4, jnp.minimum(depth + 2, 4), 1, 0)
+    weights(early, greeting)
     for load in loads[12:]:
         load.wait()
     near_experts(7, 1)
-    weights(early, stages[0])
+    weights(greeting, stages[0])
     take_rows(1)
     take_cross(0)
 

time: 123 us -> 121 us (0.984); the launches traced: 123 us -> 119 us
  Pallas kernels: 121 us -> 117 us
    pallas_call x1, Pallas kernels: 121 us -> 117 us  [layer(): pl.pallas_call(layer_kernel, out_shape=jax.ShapeDtypeStruct((tokens, widt...]
where the time goes in v5:
time: 121 us; the launch traced here: 119 us
  Pallas kernels  117 us (97%)
  local copies, waits for them, and re-layouts  1.88 us (2%)
    pallas_call x1, Pallas kernels, layer(): pl.pallas_call(layer_kernel, out_shape=jax.ShapeDtypeStruct((tokens, widt...  117 us

profile of v5, /device:TPU:1, one launch (start us, length us, event | category | flops | bytes accessed | tf_op | source)
XLA Modules:
  0.0 119.2 jit_solution(12511732619990740702)
XLA Ops:
  0.0 117.3 %shard_map.136 = bf16[128,2048]{1,0:T(8,128)(2,1)} custom-call(bf16[128,1024]{1,0:T(8,128)(2,1)} %bitcast.24, bf16[128,1024]{1,0:T(8,128)(2,1)} %bitcast.25, bf16[128,2048]{1,0:T(8,128)(2,1)} %bitcast.21, bf16[128,2048]{1,0:T(8,128)(2,1)} %bitcast.22, f32[16,128]{1,0:T(8,128)} %bitcast.27, f32[16,128]{1,0:T(8,128)} %bitcast.28, bf16[128,2048]{1,0:T(8,128)(2,1)} %bitcast.23, ...), custom_call_target="tpu_custom_call" | custom-call | tf_op jit(solution)/shard_map/pallas_call | solution.py:678
  117.3 1.9 %copy.16 = bf16[1,128,2048]{2,1,0:T(8,128)(2,1)} copy(bf16[1,128,2048]{2,1,0:T(8,128)(2,1)} %bitcast.20) | data formatting | bytes 1048576

commit v6 on v5

--- a/solution.py
+++ b/solution.py
@@ -554,7 +554,7 @@
 
     send_rows(0, 0)
     send_rows(0, 1)
-    greeting = (depth + 4, jnp.minimum(depth + 2, 4), 1, 0)
+    greeting = (depth + 4, depth + 1, 1, 0)
     weights(early, greeting)
     for load in loads[12:]:
         load.wait()

time: 121 us -> 121 us (level)
  no operation moved by 1% of the time
where the time goes in v6:
time: 121 us; the launch traced here: 119 us
  Pallas kernels  117 us (97%)
  local copies, waits for them, and re-layouts  1.88 us (2%)
    pallas_call x1, Pallas kernels, layer(): pl.pallas_call(layer_kernel, out_shape=jax.ShapeDtypeStruct((tokens, widt...  117 us

profile of v6, /device:TPU:1, one launch (start us, length us, event | category | flops | bytes accessed | tf_op | source)
XLA Modules:
  0.0 119.2 jit_solution(16908840324815351279)
XLA Ops:
  0.0 117.3 %shard_map.136 = bf16[128,2048]{1,0:T(8,128)(2,1)} custom-call(bf16[128,1024]{1,0:T(8,128)(2,1)} %bitcast.24, bf16[128,1024]{1,0:T(8,128)(2,1)} %bitcast.25, bf16[128,2048]{1,0:T(8,128)(2,1)} %bitcast.21, bf16[128,2048]{1,0:T(8,128)(2,1)} %bitcast.22, f32[16,128]{1,0:T(8,128)} %bitcast.27, f32[16,128]{1,0:T(8,128)} %bitcast.28, bf16[128,2048]{1,0:T(8,128)(2,1)} %bitcast.23, ...), custom_call_target="tpu_custom_call" | custom-call | tf_op jit(solution)/shard_map/pallas_call | solution.py:678
  117.3 1.9 %copy.16 = bf16[1,128,2048]{2,1,0:T(8,128)(2,1)} copy(bf16[1,128,2048]{2,1,0:T(8,128)(2,1)} %bitcast.20) | data formatting | bytes 1048576
